TPU v7x, 256 devices: a whole 4x4x8 slice. The times are simulated.
256 devices in a mesh: gx: 64 (over y, x, z_hi), gy: 4 (over z_lo, core).
Axes of the slice: x: 4, y: 4, z: 8 (z_hi: 4, z_lo: 2; z = z_hi * 2 + z_lo), core: 2. Of those that a mesh axis runs over, the one named last changes fastest.
Arguments:
- query_feats: bfloat16 [64, 4, 512, 768], P('gx', 'gy'), may hold values from -16 to 16
- anchors: bfloat16 [128, 8, 128, 768], P('gx', 'gy'), may hold values from -16 to 16
- tile_lists: int32 [64, 4, 4, 4], P('gx', 'gy'), may hold values from 0 to 15, as said below
- tile_counts: int32 [64, 4, 4], P('gx', 'gy'), may hold values from 1 to 4, as said below
- out_grad: bfloat16 [64, 4, 512, 768], P('gx', 'gy'), may hold values from -6 to 6
- w_query: bfloat16 [768, 768], replicated, may hold values from -0.21875 to 0.21875
- w_key: bfloat16 [768, 768], replicated, may hold values from -0.21875 to 0.21875
- w_value: bfloat16 [768, 768], replicated, may hold values from -0.21875 to 0.21875
- w_out: bfloat16 [768, 768], replicated, may hold values from -0.21875 to 0.21875
Outputs:
- query_grad: bfloat16 [64, 4, 512, 768], P('gx', 'gy')
- anchor_grad: bfloat16 [128, 8, 128, 768], P('gx', 'gy')
- weight_grads: float32 [3072, 768], P(('gx', 'gy'))
Inputs may be any that keep to these rules, and one draw needn't show every extreme that they name: `tile_lists`: within one block the 4 entries are distinct, and each names a window tile that lies inside the grid. `tile_counts`: every brick has a level; its first block's count equals the level and no count of the brick exceeds it. Some brick's level is 4.
All inputs are finite; a program needn't handle non-finite values.
Results may differ from a plain program's by a relative error of at most 0.029.
The roundings to bfloat16 on the way count: a program that leaves them out, or rounds other values in their place, can miss the bound.
Values may be sent and summed in bfloat16 or wider, within the bound.
A program may use at most 192 MiB of HBM per device.

v0:
```python
from functools import partial

import jax
import jax.numpy as jnp
from jax import lax
from jax.sharding import PartitionSpec as P

HEADS = 12
HEAD_DIM = 64
KT = 4


def from_behind(shard, axis, by):
    devices = lax.axis_size(axis)
    pairs = [(i, i + by) for i in range(devices) if 0 <= i + by < devices]
    return lax.ppermute(shard, axis, pairs)


def padded(cells, sides, width):
    for axis, dim in sides:
        count = lax.axis_size(axis)
        ends = count - 1
        head = lax.slice_in_dim(cells, 0, width, axis=dim)
        tail = lax.slice_in_dim(cells, cells.shape[dim] - width, cells.shape[dim], axis=dim)
        cells = jnp.concatenate(
            [
                lax.ppermute(tail, axis, [(i, (i + 1) % count) for i in range(ends)]),
                cells,
                lax.ppermute(head, axis, [((i + 1) % count, i) for i in range(ends)]),
            ],
            axis=dim,
        )
    return cells


def contract_rows(left, right):
    return lax.dot_general(
        left, right, (((0,), (0,)), ((), ())), preferred_element_type=jnp.float32
    )


def times_transpose(left, right):
    return lax.dot_general(
        left, right, (((1,), (1,)), ((), ())), preferred_element_type=jnp.float32
    )


def attention_step(window_flat, carry, inputs):
    query_blk, dout_blk, list_blk, count_blk = inputs
    per_step = list_blk.shape[0]
    tile_len = window_flat.shape[1]
    width = window_flat.shape[-1] // 2
    key_count = KT * tile_len
    picked = window_flat[list_blk.reshape(-1)].reshape(per_step, key_count, 2 * width)
    key_blk = picked[:, :, :width].reshape(per_step, key_count, HEADS, HEAD_DIM)
    value_blk = picked[:, :, width:].reshape(per_step, key_count, HEADS, HEAD_DIM)
    scale = HEAD_DIM ** (-0.5)
    scores = (
        jnp.einsum("bqhd,bkhd->bhqk", query_blk, key_blk, preferred_element_type=jnp.float32)
        * scale
    )
    slot_of = lax.broadcasted_iota(jnp.int32, (1, key_count), 1) // tile_len
    live = slot_of < count_blk[:, None]
    scores = jnp.where(live[:, None, None, :], scores, -jnp.inf)
    row_max = jnp.max(scores, axis=-1, keepdims=True)
    expo_vals = jnp.exp(scores - row_max)
    prob_full = expo_vals / jnp.sum(expo_vals, axis=-1, keepdims=True)
    prob_half = prob_full.astype(jnp.bfloat16)
    attended = jnp.einsum(
        "bhqk,bkhd->bqhd", prob_half, value_blk, preferred_element_type=jnp.float32
    ).astype(jnp.bfloat16)
    dprob = jnp.einsum("bqhd,bkhd->bhqk", dout_blk, value_blk, preferred_element_type=jnp.float32)
    row_delta = jnp.einsum("bqhd,bqhd->bhq", dout_blk, attended, preferred_element_type=jnp.float32)
    dscore = (prob_full * (dprob - row_delta[..., None])).astype(jnp.bfloat16)
    dquery = (
        jnp.einsum("bhqk,bkhd->bqhd", dscore, key_blk, preferred_element_type=jnp.float32) * scale
    ).astype(jnp.bfloat16)
    dkey = (
        jnp.einsum("bhqk,bqhd->bkhd", dscore, query_blk, preferred_element_type=jnp.float32) * scale
    )
    dvalue = jnp.einsum("bhqk,bqhd->bkhd", prob_half, dout_blk, preferred_element_type=jnp.float32)
    slot_grads = jnp.concatenate(
        [
            dkey.reshape(per_step * KT, tile_len, width),
            dvalue.reshape(per_step * KT, tile_len, width),
        ],
        axis=-1,
    ).reshape(per_step * KT, tile_len * 2 * width)
    tiles = window_flat.shape[0]
    selector = (
        lax.broadcasted_iota(jnp.int32, (tiles, per_step * KT), 0) == list_blk.reshape(1, -1)
    ).astype(jnp.float32)
    added = jnp.dot(
        selector, slot_grads, precision=lax.Precision.HIGHEST, preferred_element_type=jnp.float32
    )
    carry = carry + added.reshape(carry.shape)
    return (
        carry,
        (dquery.reshape(per_step * tile_len, width), attended.reshape(per_step * tile_len, width)),
    )


def return_direct(partial_half):
    span_x = partial_half.shape[0] - 2
    span_y = partial_half.shape[1] - 2
    across = lax.axis_size("gy")
    place_y = lax.axis_index("gy")
    total = partial_half[1:-1, 1:-1].astype(jnp.float32)
    source_rows = {-1: (0, 1), 0: (1, span_x + 1), 1: (span_x + 1, span_x + 2)}
    source_cols = {-1: (0, 1), 0: (1, span_y + 1), 1: (span_y + 1, span_y + 2)}
    target_rows = {-1: (span_x - 1, span_x), 0: (0, span_x), 1: (0, 1)}
    target_cols = {-1: (span_y - 1, span_y), 0: (0, span_y), 1: (0, 1)}
    for step_x in (-1, 0, 1):
        for step_y in (-1, 0, 1):
            if step_x == 0 and step_y == 0:
                continue
            row_lo, row_hi = source_rows[step_x]
            col_lo, col_hi = source_cols[step_y]
            piece = partial_half[row_lo:row_hi, col_lo:col_hi]
            arrived = from_behind(piece, ("gx", "gy"), step_x * across + step_y)
            keeping = (place_y - step_y >= 0) & (place_y - step_y < across)
            arrived = jnp.where(keeping, arrived.astype(jnp.float32), 0.0)
            goal_lo, goal_hi = target_rows[step_x]
            aim_lo, aim_hi = target_cols[step_y]
            total = total.at[goal_lo:goal_hi, aim_lo:aim_hi].add(arrived)
    return total


def on_device(
    query_feats, anchors, tile_lists, tile_counts, out_grad, w_query, w_key, w_value, w_out
):
    span_x, span_y, tile_len, width = anchors.shape
    queries_in = query_feats.reshape(-1, width)
    dout_in = out_grad.reshape(-1, width)
    lists = tile_lists.reshape(-1, KT)
    counts = tile_counts.reshape(-1)
    w_pair = jnp.concatenate([w_key, w_value], axis=1)
    pairs = jnp.dot(anchors.reshape(-1, width), w_pair, preferred_element_type=jnp.float32)
    pairs = pairs.astype(jnp.bfloat16).reshape(span_x, span_y, tile_len, 2 * width)
    window = padded(pairs, (("gx", 0), ("gy", 1)), 1)
    window_flat = window.reshape(-1, tile_len, 2 * width)
    query_proj = jnp.dot(queries_in, w_query, preferred_element_type=jnp.float32).astype(
        jnp.bfloat16
    )
    dout_proj = times_transpose(dout_in, w_out).astype(jnp.bfloat16)
    blocks = lists.shape[0]
    per_step = 2
    rounds = blocks // per_step
    stacked = (
        query_proj.reshape(rounds, per_step, tile_len, HEADS, HEAD_DIM),
        dout_proj.reshape(rounds, per_step, tile_len, HEADS, HEAD_DIM),
        lists.reshape(rounds, per_step, KT),
        counts.reshape(rounds, per_step),
    )
    start = jnp.zeros((window_flat.shape[0], tile_len, 2 * width), jnp.float32)
    partial_sum, (dquery, attended) = lax.scan(partial(attention_step, window_flat), start, stacked)
    dquery = dquery.reshape(-1, width)
    attended = attended.reshape(-1, width)
    partial_half = partial_sum.reshape(window.shape).astype(jnp.bfloat16)
    total = return_direct(partial_half)
    pair_grads = total.astype(jnp.bfloat16).reshape(-1, 2 * width)
    anchor_grad = times_transpose(pair_grads, w_pair).astype(jnp.bfloat16).reshape(anchors.shape)
    query_grad = times_transpose(dquery, w_query).astype(jnp.bfloat16).reshape(query_feats.shape)
    grad_pair_w = contract_rows(anchors.reshape(-1, width), pair_grads)
    grad_query_w = contract_rows(queries_in, dquery)
    grad_out_w = contract_rows(attended, dout_in)
    normalizer = (lax.axis_size("gx") * lax.axis_size("gy") * queries_in.shape[0]) ** (-0.5)
    terms = (
        jnp.concatenate(
            [grad_query_w, grad_pair_w[:, :width], grad_pair_w[:, width:], grad_out_w], axis=0
        )
        * normalizer
    )
    weight_grads = lax.psum_scatter(terms, ("gx", "gy"), scatter_dimension=0, tiled=True)
    return (query_grad, anchor_grad, weight_grads)


def solution(mesh):
    in_specs = (
        P("gx", "gy", None, None),
        P("gx", "gy", None, None),
        P("gx", "gy", None, None),
        P("gx", "gy", None),
        P("gx", "gy", None, None),
        P(),
        P(),
        P(),
        P(),
    )
    out_specs = (P("gx", "gy", None, None), P("gx", "gy", None, None), P(("gx", "gy"), None))
    return jax.shard_map(
        on_device, mesh=mesh, in_specs=in_specs, out_specs=out_specs, check_vma=False
    )
```

profile of v0, /device:TPU:1, one launch (start us, length us, event | category | flops | bytes accessed | tf_op | source)
XLA Modules:
  0.0 1734.7 jit_solution(18400594162277935106)
XLA Ops:
  11.2 20.2 %collective-permute-done = bf16[1,2,128,1536]{3,2,1,0:T(8,128)(2,1)S(1)} collective-permute-done((bf16[1,2,128,1536]{3,2,1,0:T(8,128)(2,1)S(1)}, bf16[1,2,128,1536]{3,2,1,0:T(8,128)(2,1)S(1)}, u32[]{:S(2)}, u32[]{:S(2)}) %collective-permute-start) | collective-permute-done | bytes 786464 | tf_op jit(solution)/shard_map/ppermute | solution.py:27
  31.4 18.9 %collective-permute-done.1 = bf16[1,2,128,1536]{3,2,1,0:T(8,128)(2,1)S(1)} collective-permute-done((bf16[1,2,128,1536]{3,2,1,0:T(8,128)(2,1)S(1)}, bf16[1,2,128,1536]{3,2,1,0:T(8,128)(2,1)S(1)}, u32[]{:S(2)}, u32[]{:S(2)}) %collective-permute-start.1) | collective-permute-done | bytes 786464 | tf_op jit(solution)/shard_map/ppermute | solution.py:29
  82.6 182.3 %while.25 = (s32[]{:T(128)}, f32[16,128,1536]{2,0,1:T(8,128)}, bf16[2,256,768]{2,1,0:T(8,128)(2,1)}, bf16[2,256,768]{2,1,0:T(8,128)(2,1)}, s32[2,2,4]{2,1,0:T(2,...) while((s32[]{:T(128)}, f32[16,128,1536]{2,0,1:T(8,128)}, ...), condition=%wide.region_3.4_spmd.clone, body=%wide.region_0.3_spmd.clone.sunk | while | flops 1535708800 | bytes 199433776 | solution.py:156
  159.4 13.2 select_add_fusion.2
  249.2 15.3 select_add_fusion.2
  264.9 8.2 convert_element_type.90
  280.1 12.5 collective-permute-start.4
  293.9 14.3 collective-permute-start.6
  308.3 13.8 collective-permute-start.7
  327.4 12.2 collective-permute-start.9
  339.9 11.4 collective-permute-done.5
  358.0 11.4 collective-permute-start.11
  371.8 14.3 collective-permute-done.10
  386.6 19.8 %collective-permute-done.11 = bf16[1,1,128,1536]{3,2,1,0:T(8,128)(2,1)S(1)} collective-permute-done((bf16[1,1,128,1536]{3,2,1,0:T(8,128)(2,1)S(1)}, bf16[1,1,128,1536]{3,2,1,0:T(8,128)(2,1)S(1)}, u32[]{:S(2)}, u32[]{:S(2)}) %collective-permute-start.11) | collective-permute-done | bytes 393248 | tf_op jit(solution)/shard_map/ppermute | solution.py:16
  413.6 718.7 %fusion = f32[16,768]{1,0:T(8,128)} fusion(f32[3072,768]{1,0:T(8,128)} %maximum_multiply_fusion), kind=kCustom, calls=%all-reduce-scatter | all-reduce-scatter fusion | flops 3145729 | bytes 9486336
  1155.9 9.2 collective-permute-start.17
  1165.1 13.1 collective-permute-start.18
  1178.2 13.1 collective-permute-start.19
  1191.3 13.1 collective-permute-start.20
  1204.5 13.1 collective-permute-start.21
  1217.6 13.2 collective-permute-start.22
  1230.8 13.1 collective-permute-start.23
  1243.9 13.1 collective-permute-start.24
  1257.0 13.1 collective-permute-start.25
  1270.2 13.1 collective-permute-start.26
  1283.3 13.1 collective-permute-start.27
  1296.5 13.1 collective-permute-start.28
  1309.6 13.1 collective-permute-start.29
  1322.7 13.2 collective-permute-start.30
  1335.9 13.1 collective-permute-start.31
  1349.0 13.1 collective-permute-start.32
  1362.2 13.1 collective-permute-start.33
  1375.3 13.1 collective-permute-start.34
  1388.5 13.1 collective-permute-start.35
  1401.6 13.1 collective-permute-start.36
  1414.7 13.1 collective-permute-start.37
  1427.9 13.1 collective-permute-start.38
  1441.0 13.1 collective-permute-start.39
  1454.2 13.1 collective-permute-start.40
  1467.3 13.1 collective-permute-start.41
  1480.4 13.1 collective-permute-start.42
  1493.6 13.1 collective-permute-start.43
  1506.7 13.1 collective-permute-start.44
  1519.9 13.1 collective-permute-start.45
  1533.0 13.1 collective-permute-start.46
  1553.2 7.5 collective-permute-start.48
  1563.7 7.5 collective-permute-start.50
  1637.6 95.4 %concatenate.41 = f32[1036,768]{1,0:T(8,128)} concatenate(f32[12,768]{1,0:T(8,128)} %collective-permute-done.75, f32[16,768]{1,0:T(8,128)S(1)} %collective-permute-done.74, f32[16,768]{1,0:T(8,128)S(1)} %collective-permute-done.73, f32[16,768]{1,0:T(8,128)S(1)} %collective-permute-done.72, f32[16,768]{1,0:T(8,128)S(1)} %collective-permute-done.71, ...), dimensions={0} | concatenate | bytes 6365184
  (294 shorter events, 327.4 us)
Async XLA Ops:
  4.1 27.3 %collective-permute-start = (bf16[1,2,128,1536]{3,2,1,0:T(8,128)(2,1)S(1)}, bf16[1,2,128,1536]{3,2,1,0:T(8,128)(2,1)S(1)}, u32[]{:S(2)}, u32[]{:S(2)}) collective-permute-start(bf16[1,2,128,1536]{3,2,1,0:T(8,128)(2,1)S(1)} %bitcast.189), channel_id=1, source_target_pairs={{0,4},{4,8},{8,12},{12,16},{16,20},{20,24},{24,28},{28,32},{32,36}... | collective-permute-start | bytes 2359304 | tf_op jit(solution)/shard_map/ppermute | solution.py:27
  9.9 40.4 %collective-permute-start.1 = (bf16[1,2,128,1536]{3,2,1,0:T(8,128)(2,1)S(1)}, bf16[1,2,128,1536]{3,2,1,0:T(8,128)(2,1)S(1)}, u32[]{:S(2)}, u32[]{:S(2)}) collective-permute-start(bf16[1,2,128,1536]{3,2,1,0:T(8,128)(2,1)S(1)} %bitcast.188), channel_id=1, source_target_pairs={{4,0},{8,4},{12,8},{16,12},{20,16},{24,20},{28,24},{32,28},{36,32}... | collective-permute-start | bytes 2359304 | tf_op jit(solution)/shard_map/ppermute | solution.py:29
  280.1 47.3 %collective-permute-start.4 = (bf16[1,1,128,1536]{3,2,1,0:T(8,128)(2,1)S(1)}, bf16[1,1,128,1536]{3,2,1,0:T(8,128)(2,1)S(1)}, u32[]{:S(2)}, u32[]{:S(2)}) collective-permute-start(bf16[1,1,128,1536]{3,2,1,0:T(8,128)(2,1)S(1)} %get-tuple-element.317), channel_id=1, source_target_pairs={{5,0},{6,1},{7,2},{8,3},{9,4},{10,5},{11,6},{12,7},{13,8},{14,9},{... | collective-permute-start | bytes 1179656 | tf_op jit(solution)/shard_map/ppermute | solution.py:16
  292.7 58.6 %collective-permute-start.5 = (bf16[1,2,128,1536]{3,2,1,0:T(8,128)(2,1)S(1)}, bf16[1,2,128,1536]{3,2,1,0:T(8,128)(2,1)S(1)}, u32[]{:S(2)}, u32[]{:S(2)}) collective-permute-start(bf16[1,2,128,1536]{3,2,1,0:T(8,128)(2,1)S(1)} %get-tuple-element.319), channel_id=1, source_target_pairs={{4,0},{5,1},{6,2},{7,3},{8,4},{9,5},{10,6},{11,7},{12,8},{13,9},{1... | collective-permute-start | bytes 2359304 | tf_op jit(solution)/shard_map/ppermute | solution.py:16
  293.9 64.1 %collective-permute-start.6 = (bf16[1,1,128,1536]{3,2,1,0:T(8,128)(2,1)S(1)}, bf16[1,1,128,1536]{3,2,1,0:T(8,128)(2,1)S(1)}, u32[]{:S(2)}, u32[]{:S(2)}) collective-permute-start(bf16[1,1,128,1536]{3,2,1,0:T(8,128)(2,1)S(1)} %get-tuple-element.316), channel_id=1, source_target_pairs={{3,0},{4,1},{5,2},{6,3},{7,4},{8,5},{9,6},{10,7},{11,8},{12,9},{13... | collective-permute-start | bytes 1179656 | tf_op jit(solution)/shard_map/ppermute | solution.py:16
  308.3 61.3 %collective-permute-start.7 = (bf16[2,1,128,1536]{3,2,1,0:T(8,128)(2,1)S(1)}, bf16[2,1,128,1536]{3,2,1,0:T(8,128)(2,1)S(1)}, u32[]{:S(2)}, u32[]{:S(2)}) collective-permute-start(bf16[2,1,128,1536]{3,2,1,0:T(8,128)(2,1)S(1)} %get-tuple-element.321), channel_id=1, source_target_pairs={{1,0},{2,1},{3,2},{4,3},{5,4},{6,5},{7,6},{8,7},{9,8},{10,9},{11,1... | collective-permute-start | bytes 2359304 | tf_op jit(solution)/shard_map/ppermute | solution.py:16
  322.0 47.9 %collective-permute-start.8 = (bf16[2,1,128,1536]{3,2,1,0:T(8,128)(2,1)S(1)}, bf16[2,1,128,1536]{3,2,1,0:T(8,128)(2,1)S(1)}, u32[]{:S(2)}, u32[]{:S(2)}) collective-permute-start(bf16[2,1,128,1536]{3,2,1,0:T(8,128)(2,1)S(1)} %get-tuple-element.320), channel_id=1, source_target_pairs={{0,1},{1,2},{2,3},{3,4},{4,5},{5,6},{6,7},{7,8},{8,9},{9,10},{10,1... | collective-permute-start | bytes 2359304 | tf_op jit(solution)/shard_map/ppermute | solution.py:16
  327.4 42.9 %collective-permute-start.9 = (bf16[1,1,128,1536]{3,2,1,0:T(8,128)(2,1)S(1)}, bf16[1,1,128,1536]{3,2,1,0:T(8,128)(2,1)S(1)}, u32[]{:S(2)}, u32[]{:S(2)}) collective-permute-start(bf16[1,1,128,1536]{3,2,1,0:T(8,128)(2,1)S(1)} %get-tuple-element.315), channel_id=1, source_target_pairs={{0,3},{1,4},{2,5},{3,6},{4,7},{5,8},{6,9},{7,10},{8,11},{9,12},{10... | collective-permute-start | bytes 1179656 | tf_op jit(solution)/shard_map/ppermute | solution.py:16
  351.3 34.8 %collective-permute-start.10 = (bf16[1,2,128,1536]{3,2,1,0:T(8,128)(2,1)S(1)}, bf16[1,2,128,1536]{3,2,1,0:T(8,128)(2,1)S(1)}, u32[]{:S(2)}, u32[]{:S(2)}) collective-permute-start(bf16[1,2,128,1536]{3,2,1,0:T(8,128)(2,1)S(1)} %get-tuple-element.318), channel_id=1, source_target_pairs={{0,4},{1,5},{2,6},{3,7},{4,8},{5,9},{6,10},{7,11},{8,12},{9,13},{1... | collective-permute-start | bytes 2359304 | tf_op jit(solution)/shard_map/ppermute | solution.py:16
  358.0 48.3 %collective-permute-start.11 = (bf16[1,1,128,1536]{3,2,1,0:T(8,128)(2,1)S(1)}, bf16[1,1,128,1536]{3,2,1,0:T(8,128)(2,1)S(1)}, u32[]{:S(2)}, u32[]{:S(2)}) collective-permute-start(bf16[1,1,128,1536]{3,2,1,0:T(8,128)(2,1)S(1)} %get-tuple-element.314), channel_id=1, source_target_pairs={{0,5},{1,6},{2,7},{3,8},{4,9},{5,10},{6,11},{7,12},{8,13},{9,14},{... | collective-permute-start | bytes 1179656 | tf_op jit(solution)/shard_map/ppermute | solution.py:16
  1134.3 30.8 %collective-permute-start.13 = (f32[16,768]{1,0:T(8,128)}, f32[16,768]{1,0:T(8,128)}, u32[]{:S(2)}, u32[]{:S(2)}) collective-permute-start(f32[16,768]{1,0:T(8,128)} %fusion), channel_id=1, source_target_pairs={{0,2},{1,3},{2,4},{3,5},{4,6},{5,7},{6,8},{7,9},{8,10},{9,11},{10,... | collective-permute-start | bytes 147464
  1137.2 40.9 %collective-permute-start.14 = (f32[16,768]{1,0:T(8,128)}, f32[16,768]{1,0:T(8,128)}, u32[]{:S(2)}, u32[]{:S(2)}) collective-permute-start(f32[16,768]{1,0:T(8,128)} %fusion), channel_id=1, source_target_pairs={{0,3},{1,4},{2,5},{3,6},{4,7},{5,8},{6,9},{7,10},{8,11},{9,12},{10... | collective-permute-start | bytes 147464
  1146.2 45.1 %collective-permute-start.15 = (f32[16,768]{1,0:T(8,128)}, f32[16,768]{1,0:T(8,128)}, u32[]{:S(2)}, u32[]{:S(2)}) collective-permute-start(f32[16,768]{1,0:T(8,128)} %fusion), channel_id=1, source_target_pairs={{0,4},{1,5},{2,6},{3,7},{4,8},{5,9},{6,10},{7,11},{8,12},{9,13},{1... | collective-permute-start | bytes 147464
  1152.5 51.9 %collective-permute-start.16 = (f32[16,768]{1,0:T(8,128)}, f32[16,768]{1,0:T(8,128)}, u32[]{:S(2)}, u32[]{:S(2)}) collective-permute-start(f32[16,768]{1,0:T(8,128)} %fusion), channel_id=1, source_target_pairs={{0,5},{1,6},{2,7},{3,8},{4,9},{5,10},{6,11},{7,12},{8,13},{9,14},{... | collective-permute-start | bytes 147464
  1155.9 61.7 %collective-permute-start.17 = (f32[16,768]{1,0:T(8,128)}, f32[16,768]{1,0:T(8,128)}, u32[]{:S(2)}, u32[]{:S(2)}) collective-permute-start(f32[16,768]{1,0:T(8,128)} %fusion), channel_id=1, source_target_pairs={{0,6},{1,7},{2,8},{3,9},{4,10},{5,11},{6,12},{7,13},{8,14},{9,15},... | collective-permute-start | bytes 147464
  1165.1 65.7 %collective-permute-start.18 = (f32[16,768]{1,0:T(8,128)}, f32[16,768]{1,0:T(8,128)}, u32[]{:S(2)}, u32[]{:S(2)}) collective-permute-start(f32[16,768]{1,0:T(8,128)} %fusion), channel_id=1, source_target_pairs={{0,7},{1,8},{2,9},{3,10},{4,11},{5,12},{6,13},{7,14},{8,15},{9,16}... | collective-permute-start | bytes 147464
  1178.2 65.7 %collective-permute-start.19 = (f32[16,768]{1,0:T(8,128)}, f32[16,768]{1,0:T(8,128)}, u32[]{:S(2)}, u32[]{:S(2)}) collective-permute-start(f32[16,768]{1,0:T(8,128)} %fusion), channel_id=1, source_target_pairs={{0,8},{1,9},{2,10},{3,11},{4,12},{5,13},{6,14},{7,15},{8,16},{9,17... | collective-permute-start | bytes 147464
  1191.3 65.7 %collective-permute-start.20 = (f32[16,768]{1,0:T(8,128)}, f32[16,768]{1,0:T(8,128)}, u32[]{:S(2)}, u32[]{:S(2)}) collective-permute-start(f32[16,768]{1,0:T(8,128)} %fusion), channel_id=1, source_target_pairs={{0,9},{1,10},{2,11},{3,12},{4,13},{5,14},{6,15},{7,16},{8,17},{9,1... | collective-permute-start | bytes 147464
  1204.5 65.7 %collective-permute-start.21 = (f32[16,768]{1,0:T(8,128)}, f32[16,768]{1,0:T(8,128)}, u32[]{:S(2)}, u32[]{:S(2)}) collective-permute-start(f32[16,768]{1,0:T(8,128)} %fusion), channel_id=1, source_target_pairs={{0,10},{1,11},{2,12},{3,13},{4,14},{5,15},{6,16},{7,17},{8,18},{9,... | collective-permute-start | bytes 147464
  1217.6 65.7 %collective-permute-start.22 = (f32[16,768]{1,0:T(8,128)}, f32[16,768]{1,0:T(8,128)}, u32[]{:S(2)}, u32[]{:S(2)}) collective-permute-start(f32[16,768]{1,0:T(8,128)} %fusion), channel_id=1, source_target_pairs={{0,11},{1,12},{2,13},{3,14},{4,15},{5,16},{6,17},{7,18},{8,19},{9,... | collective-permute-start | bytes 147464
  1230.8 65.7 %collective-permute-start.23 = (f32[16,768]{1,0:T(8,128)}, f32[16,768]{1,0:T(8,128)}, u32[]{:S(2)}, u32[]{:S(2)}) collective-permute-start(f32[16,768]{1,0:T(8,128)} %fusion), channel_id=1, source_target_pairs={{0,12},{1,13},{2,14},{3,15},{4,16},{5,17},{6,18},{7,19},{8,20},{9,... | collective-permute-start | bytes 147464
  1243.9 65.7 %collective-permute-start.24 = (f32[16,768]{1,0:T(8,128)}, f32[16,768]{1,0:T(8,128)}, u32[]{:S(2)}, u32[]{:S(2)}) collective-permute-start(f32[16,768]{1,0:T(8,128)} %fusion), channel_id=1, source_target_pairs={{0,13},{1,14},{2,15},{3,16},{4,17},{5,18},{6,19},{7,20},{8,21},{9,... | collective-permute-start | bytes 147464
  1257.0 65.7 %collective-permute-start.25 = (f32[16,768]{1,0:T(8,128)}, f32[16,768]{1,0:T(8,128)}, u32[]{:S(2)}, u32[]{:S(2)}) collective-permute-start(f32[16,768]{1,0:T(8,128)} %fusion), channel_id=1, source_target_pairs={{0,14},{1,15},{2,16},{3,17},{4,18},{5,19},{6,20},{7,21},{8,22},{9,... | collective-permute-start | bytes 147464
  1270.2 65.7 %collective-permute-start.26 = (f32[16,768]{1,0:T(8,128)}, f32[16,768]{1,0:T(8,128)}, u32[]{:S(2)}, u32[]{:S(2)}) collective-permute-start(f32[16,768]{1,0:T(8,128)} %fusion), channel_id=1, source_target_pairs={{0,15},{1,16},{2,17},{3,18},{4,19},{5,20},{6,21},{7,22},{8,23},{9,... | collective-permute-start | bytes 147464
  1283.3 65.7 %collective-permute-start.27 = (f32[16,768]{1,0:T(8,128)}, f32[16,768]{1,0:T(8,128)}, u32[]{:S(2)}, u32[]{:S(2)}) collective-permute-start(f32[16,768]{1,0:T(8,128)} %fusion), channel_id=1, source_target_pairs={{0,16},{1,17},{2,18},{3,19},{4,20},{5,21},{6,22},{7,23},{8,24},{9,... | collective-permute-start | bytes 147464
  1296.5 65.7 %collective-permute-start.28 = (f32[16,768]{1,0:T(8,128)}, f32[16,768]{1,0:T(8,128)}, u32[]{:S(2)}, u32[]{:S(2)}) collective-permute-start(f32[16,768]{1,0:T(8,128)} %fusion), channel_id=1, source_target_pairs={{0,17},{1,18},{2,19},{3,20},{4,21},{5,22},{6,23},{7,24},{8,25},{9,... | collective-permute-start | bytes 147464
  1309.6 65.7 %collective-permute-start.29 = (f32[16,768]{1,0:T(8,128)}, f32[16,768]{1,0:T(8,128)}, u32[]{:S(2)}, u32[]{:S(2)}) collective-permute-start(f32[16,768]{1,0:T(8,128)} %fusion), channel_id=1, source_target_pairs={{0,18},{1,19},{2,20},{3,21},{4,22},{5,23},{6,24},{7,25},{8,26},{9,... | collective-permute-start | bytes 147464
  1322.7 65.7 %collective-permute-start.30 = (f32[16,768]{1,0:T(8,128)}, f32[16,768]{1,0:T(8,128)}, u32[]{:S(2)}, u32[]{:S(2)}) collective-permute-start(f32[16,768]{1,0:T(8,128)} %fusion), channel_id=1, source_target_pairs={{0,19},{1,20},{2,21},{3,22},{4,23},{5,24},{6,25},{7,26},{8,27},{9,... | collective-permute-start | bytes 147464
  1335.9 65.7 %collective-permute-start.31 = (f32[16,768]{1,0:T(8,128)}, f32[16,768]{1,0:T(8,128)}, u32[]{:S(2)}, u32[]{:S(2)}) collective-permute-start(f32[16,768]{1,0:T(8,128)} %fusion), channel_id=1, source_target_pairs={{0,20},{1,21},{2,22},{3,23},{4,24},{5,25},{6,26},{7,27},{8,28},{9,... | collective-permute-start | bytes 147464
  1349.0 65.7 %collective-permute-start.32 = (f32[16,768]{1,0:T(8,128)}, f32[16,768]{1,0:T(8,128)}, u32[]{:S(2)}, u32[]{:S(2)}) collective-permute-start(f32[16,768]{1,0:T(8,128)} %fusion), channel_id=1, source_target_pairs={{0,21},{1,22},{2,23},{3,24},{4,25},{5,26},{6,27},{7,28},{8,29},{9,... | collective-permute-start | bytes 147464
  1362.2 65.7 %collective-permute-start.33 = (f32[16,768]{1,0:T(8,128)}, f32[16,768]{1,0:T(8,128)}, u32[]{:S(2)}, u32[]{:S(2)}) collective-permute-start(f32[16,768]{1,0:T(8,128)} %fusion), channel_id=1, source_target_pairs={{0,22},{1,23},{2,24},{3,25},{4,26},{5,27},{6,28},{7,29},{8,30},{9,... | collective-permute-start | bytes 147464
  1375.3 65.7 %collective-permute-start.34 = (f32[16,768]{1,0:T(8,128)}, f32[16,768]{1,0:T(8,128)}, u32[]{:S(2)}, u32[]{:S(2)}) collective-permute-start(f32[16,768]{1,0:T(8,128)} %fusion), channel_id=1, source_target_pairs={{0,23},{1,24},{2,25},{3,26},{4,27},{5,28},{6,29},{7,30},{8,31},{9,... | collective-permute-start | bytes 147464
  1388.5 65.7 %collective-permute-start.35 = (f32[16,768]{1,0:T(8,128)}, f32[16,768]{1,0:T(8,128)}, u32[]{:S(2)}, u32[]{:S(2)}) collective-permute-start(f32[16,768]{1,0:T(8,128)} %fusion), channel_id=1, source_target_pairs={{0,24},{1,25},{2,26},{3,27},{4,28},{5,29},{6,30},{7,31},{8,32},{9,... | collective-permute-start | bytes 147464
  1401.6 65.7 %collective-permute-start.36 = (f32[16,768]{1,0:T(8,128)}, f32[16,768]{1,0:T(8,128)}, u32[]{:S(2)}, u32[]{:S(2)}) collective-permute-start(f32[16,768]{1,0:T(8,128)} %fusion), channel_id=1, source_target_pairs={{0,25},{1,26},{2,27},{3,28},{4,29},{5,30},{6,31},{7,32},{8,33},{9,... | collective-permute-start | bytes 147464
  1414.7 65.7 %collective-permute-start.37 = (f32[16,768]{1,0:T(8,128)}, f32[16,768]{1,0:T(8,128)}, u32[]{:S(2)}, u32[]{:S(2)}) collective-permute-start(f32[16,768]{1,0:T(8,128)} %fusion), channel_id=1, source_target_pairs={{0,26},{1,27},{2,28},{3,29},{4,30},{5,31},{6,32},{7,33},{8,34},{9,... | collective-permute-start | bytes 147464
  1427.9 65.7 %collective-permute-start.38 = (f32[16,768]{1,0:T(8,128)}, f32[16,768]{1,0:T(8,128)}, u32[]{:S(2)}, u32[]{:S(2)}) collective-permute-start(f32[16,768]{1,0:T(8,128)} %fusion), channel_id=1, source_target_pairs={{0,27},{1,28},{2,29},{3,30},{4,31},{5,32},{6,33},{7,34},{8,35},{9,... | collective-permute-start | bytes 147464
  1441.0 65.7 %collective-permute-start.39 = (f32[16,768]{1,0:T(8,128)}, f32[16,768]{1,0:T(8,128)}, u32[]{:S(2)}, u32[]{:S(2)}) collective-permute-start(f32[16,768]{1,0:T(8,128)} %fusion), channel_id=1, source_target_pairs={{0,28},{1,29},{2,30},{3,31},{4,32},{5,33},{6,34},{7,35},{8,36},{9,... | collective-permute-start | bytes 147464
  1454.2 65.7 %collective-permute-start.40 = (f32[16,768]{1,0:T(8,128)}, f32[16,768]{1,0:T(8,128)}, u32[]{:S(2)}, u32[]{:S(2)}) collective-permute-start(f32[16,768]{1,0:T(8,128)} %fusion), channel_id=1, source_target_pairs={{0,29},{1,30},{2,31},{3,32},{4,33},{5,34},{6,35},{7,36},{8,37},{9,... | collective-permute-start | bytes 147464
  1467.3 65.7 %collective-permute-start.41 = (f32[16,768]{1,0:T(8,128)}, f32[16,768]{1,0:T(8,128)}, u32[]{:S(2)}, u32[]{:S(2)}) collective-permute-start(f32[16,768]{1,0:T(8,128)} %fusion), channel_id=1, source_target_pairs={{0,30},{1,31},{2,32},{3,33},{4,34},{5,35},{6,36},{7,37},{8,38},{9,... | collective-permute-start | bytes 147464
  1480.4 65.7 %collective-permute-start.42 = (f32[16,768]{1,0:T(8,128)}, f32[16,768]{1,0:T(8,128)}, u32[]{:S(2)}, u32[]{:S(2)}) collective-permute-start(f32[16,768]{1,0:T(8,128)} %fusion), channel_id=1, source_target_pairs={{0,31},{1,32},{2,33},{3,34},{4,35},{5,36},{6,37},{7,38},{8,39},{9,... | collective-permute-start | bytes 147464
  1493.6 59.6 %collective-permute-start.43 = (f32[16,768]{1,0:T(8,128)}, f32[16,768]{1,0:T(8,128)}, u32[]{:S(2)}, u32[]{:S(2)}) collective-permute-start(f32[16,768]{1,0:T(8,128)} %fusion), channel_id=1, source_target_pairs={{0,32},{1,33},{2,34},{3,35},{4,36},{5,37},{6,38},{7,39},{8,40},{9,... | collective-permute-start | bytes 147464
  1506.7 54.0 %collective-permute-start.44 = (f32[16,768]{1,0:T(8,128)}, f32[16,768]{1,0:T(8,128)}, u32[]{:S(2)}, u32[]{:S(2)}) collective-permute-start(f32[16,768]{1,0:T(8,128)} %fusion), channel_id=1, source_target_pairs={{0,33},{1,34},{2,35},{3,36},{4,37},{5,38},{6,39},{7,40},{8,41},{9,... | collective-permute-start | bytes 147464
  1519.9 43.9 %collective-permute-start.45 = (f32[16,768]{1,0:T(8,128)}, f32[16,768]{1,0:T(8,128)}, u32[]{:S(2)}, u32[]{:S(2)}) collective-permute-start(f32[16,768]{1,0:T(8,128)} %fusion), channel_id=1, source_target_pairs={{0,34},{1,35},{2,36},{3,37},{4,38},{5,39},{6,40},{7,41},{8,42},{9,... | collective-permute-start | bytes 147464
  1533.0 38.3 %collective-permute-start.46 = (f32[16,768]{1,0:T(8,128)}, f32[16,768]{1,0:T(8,128)}, u32[]{:S(2)}, u32[]{:S(2)}) collective-permute-start(f32[16,768]{1,0:T(8,128)} %fusion), channel_id=1, source_target_pairs={{0,35},{1,36},{2,37},{3,38},{4,39},{5,40},{6,41},{7,42},{8,43},{9,... | collective-permute-start | bytes 147464
  1546.2 31.5 %collective-permute-start.47 = (f32[16,768]{1,0:T(8,128)}, f32[16,768]{1,0:T(8,128)}, u32[]{:S(2)}, u32[]{:S(2)}) collective-permute-start(f32[16,768]{1,0:T(8,128)} %fusion), channel_id=1, source_target_pairs={{0,36},{1,37},{2,38},{3,39},{4,40},{5,41},{6,42},{7,43},{8,44},{9,... | collective-permute-start | bytes 147464
  1553.2 31.2 %collective-permute-start.48 = (f32[16,768]{1,0:T(8,128)}, f32[16,768]{1,0:T(8,128)}, u32[]{:S(2)}, u32[]{:S(2)}) collective-permute-start(f32[16,768]{1,0:T(8,128)} %fusion), channel_id=1, source_target_pairs={{0,37},{1,38},{2,39},{3,40},{4,41},{5,42},{6,43},{7,44},{8,45},{9,... | collective-permute-start | bytes 147464
  1560.7 25.6 %collective-permute-start.49 = (f32[16,768]{1,0:T(8,128)}, f32[16,768]{1,0:T(8,128)}, u32[]{:S(2)}, u32[]{:S(2)}) collective-permute-start(f32[16,768]{1,0:T(8,128)} %fusion), channel_id=1, source_target_pairs={{0,38},{1,39},{2,40},{3,41},{4,42},{5,43},{6,44},{7,45},{8,46},{9,... | collective-permute-start | bytes 147464
  1563.7 24.4 %collective-permute-start.50 = (f32[16,768]{1,0:T(8,128)}, f32[16,768]{1,0:T(8,128)}, u32[]{:S(2)}, u32[]{:S(2)}) collective-permute-start(f32[16,768]{1,0:T(8,128)} %fusion), channel_id=1, source_target_pairs={{0,39},{1,40},{2,41},{3,42},{4,43},{5,44},{6,45},{7,46},{8,47},{9,... | collective-permute-start | bytes 147464
  (64 other events, 779.9 us)
where the time goes:
time: 1750 us; the launch traced here: 1730 us
  blocking collectives  719 us (41%)
  starting transfers between devices  588 us (34%)
  local copies, waits for them, and re-layouts  219 us (13%)
  waiting for transfers between devices  84.9 us (5%)
  matrix products  79.4 us (5%)
  other arithmetic  42.7 us (2%)
    unnamed x1, blocking collectives  719 us
    unnamed x64, starting transfers between devices  500 us
    unnamed x53, local copies, waits for them, and re-layouts  102 us
    ppermute x8, starting transfers between devices, from_behind(): return lax.ppermute(shard, axis, pairs)  75.4 us
    ppermute x8, waiting for transfers between devices, from_behind(): return lax.ppermute(shard, axis, pairs)  45.5 us
  transfers between devices with their start and end apart: 76, of which 5 were waited for; matrix products, arithmetic and copies ran while one was open for 2% of the time, Pallas kernels for 0%

commit v1 on v0

v1 whole, which is shorter than its diff:
```python
from functools import partial

import jax
import jax.numpy as jnp
from jax import lax
from jax.experimental import pallas as pl
from jax.experimental.pallas import tpu as pltpu
from jax.sharding import PartitionSpec as P

HEADS = 12
HEAD_DIM = 64
KT = 4
D = 768
TILE = 128
PAIRS = 6
Q_DEV = 512
SCALE = HEAD_DIM ** (-0.5)
HALF = 384
NEG = -1e30
MESH = pl.DeviceIdType.MESH
F32 = jnp.float32
BF16 = jnp.bfloat16
VMEM_BYTES = 56 * 1024 * 1024

DIRS = ((-1, 0), (1, 0), (-1, -1), (-1, 1), (1, -1), (1, 1), (0, -1), (0, 1))
OWN = {-1: (0, 1), 0: (0, 2), 1: (1, 2)}
LAND = {-1: (3, 4), 0: (1, 3), 1: (0, 1)}
ROWS = {-1: (1,), 0: (0, 1), 1: (0,)}


def nn(left, right):
    return lax.dot_general(left, right, (((1,), (0,)), ((), ())), preferred_element_type=F32)


def nt(left, right):
    return lax.dot_general(left, right, (((1,), (1,)), ((), ())), preferred_element_type=F32)


def tn(left, right):
    return lax.dot_general(left, right, (((0,), (0,)), ((), ())), preferred_element_type=F32)


def inside(place, extents):
    (px, py), (nx, ny) = place, extents
    return (px >= 0) & (px < nx) & (py >= 0) & (py < ny)


def greet(partners):
    barrier = pltpu.get_barrier_semaphore()
    total = jnp.int32(0)
    for where, present in partners:
        @pl.when(present)
        def _():
            pl.semaphore_signal(barrier, inc=1, device_id=where, device_id_type=MESH)
        total = total + jnp.where(present, 1, 0).astype(jnp.int32)
    pl.semaphore_wait(barrier, total)


def halo_kernel(
    extents,
    anchors, qf_in, do_in, wq_in, wk_in, wv_in, wo_in,
    kw_out, vw_out, awt_out, q_out, dp_out, dpt_out, qft_out,
    win, kw, vw, awt, qf, do, wq, wk, wv, wo, q_s, dp_s, dpt_s, qft_s,
    send_sem, recv_sem, load_sem, store_sem,
):
    gx, gy = lax.axis_index("gx"), lax.axis_index("gy")
    loads = [
        pltpu.make_async_copy(src, dst, load_sem.at[i])
        for i, (src, dst) in enumerate(
            [(qf_in, qf), (wq_in, wq), (do_in, do), (wo_in, wo), (wk_in, wk), (wv_in, wv)]
        )
    ]
    own = pltpu.make_async_copy(anchors, win.at[1:3, 1:3], load_sem.at[6])
    for load in loads:
        load.start()
    own.start()
    greet([((gx + dx, gy + dy), inside((gx + dx, gy + dy), extents)) for dx, dy in DIRS])

    def sending(i):
        dx, dy = DIRS[i]
        (r0, r1), (c0, c1) = OWN[dx], OWN[dy]
        (p0, p1), (q0, q1) = LAND[dx], LAND[dy]
        return pltpu.make_async_remote_copy(
            src_ref=anchors.at[r0:r1, c0:c1],
            dst_ref=win.at[p0:p1, q0:q1],
            send_sem=send_sem.at[i],
            recv_sem=recv_sem.at[i],
            device_id=(gx + dx, gy + dy),
            device_id_type=MESH,
        )

    for i, (dx, dy) in enumerate(DIRS):
        @pl.when(inside((gx + dx, gy + dy), extents))
        def _(i=i):
            sending(i).start()

    for dx, dy in DIRS:
        (p0, p1), (q0, q1) = LAND[dx], LAND[dy]

        @pl.when(jnp.logical_not(inside((gx - dx, gy - dy), extents)))
        def _(p0=p0, p1=p1, q0=q0, q1=q1):
            win[p0:p1, q0:q1] = jnp.zeros((p1 - p0, q1 - q0, TILE, D), BF16)

    loads[0].wait()
    loads[1].wait()

    def project_query(j, _):
        at = pl.ds(pl.multiple_of(j * 256, 256), 256)
        q_s[:, at] = (nn(qf[...], wq[:, at]).astype(BF16) * SCALE).astype(BF16)
        return 0

    lax.fori_loop(0, 3, project_query, 0)
    loads[2].wait()
    loads[3].wait()

    def project_dout(j, _):
        at = pl.ds(pl.multiple_of(j * 256, 256), 256)
        dp_s[:, at] = nt(do[...], wo[at, :]).astype(BF16)
        dpt_s[at, :] = nt(wo[at, :], do[...]).astype(BF16)
        qft_s[at, :] = qf[:, at].T
        return 0

    lax.fori_loop(0, 3, project_dout, 0)
    stores = []

    def store(src, dst):
        copy = pltpu.make_async_copy(src, dst, store_sem.at[len(stores)])
        copy.start()
        stores.append(copy)

    store(q_s, q_out)
    store(dp_s, dp_out)
    store(dpt_s, dpt_out)
    store(qft_s, qft_out)
    loads[4].wait()
    loads[5].wait()
    own.wait()

    def project_tiles(places):
        rows = jnp.concatenate([win[r, c] for r, c in places], axis=0)

        def step(j, _):
            at = pl.ds(pl.multiple_of(j * 256, 256), 256)
            for weight, goal in ((wk, kw), (wv, vw)):
                part = nn(rows, weight[:, at]).astype(BF16)
                for n, (r, c) in enumerate(places):
                    for i in range(2):
                        goal[2 * j + i, r * 4 + c] = part[
                            n * TILE : (n + 1) * TILE, i * TILE : (i + 1) * TILE
                        ]
            return 0

        lax.fori_loop(0, 3, step, 0)
        for r, c in places:
            awt[r * 4 + c] = win[r, c].T

    def arrive(dx, dy):
        @pl.when(inside((gx - dx, gy - dy), extents))
        def _():
            sending(DIRS.index((dx, dy))).wait_recv()

    project_tiles([(1, 1), (1, 2), (2, 1), (2, 2)])
    arrive(0, 1)
    project_tiles([(1, 0), (2, 0)])
    arrive(0, -1)
    project_tiles([(1, 3), (2, 3)])
    store(kw.at[:, 4:12], kw_out.at[:, 4:12])
    store(vw.at[:, 4:12], vw_out.at[:, 4:12])
    store(awt.at[4:12], awt_out.at[4:12])
    for dx, first in ((1, 0), (-1, 12)):
        for dy in (0, -1, 1):
            arrive(dx, dy)
        project_tiles([(first // 4, c) for c in range(4)])
        store(kw.at[:, first : first + 4], kw_out.at[:, first : first + 4])
        store(vw.at[:, first : first + 4], vw_out.at[:, first : first + 4])
        store(awt.at[first : first + 4], awt_out.at[first : first + 4])
    for i, (dx, dy) in enumerate(DIRS):
        @pl.when(inside((gx + dx, gy + dy), extents))
        def _(i=i):
            sending(i).wait_send()
    for copy in stores:
        copy.wait()


def halo(extents, anchors, qf, do, wq, wk, wv, wo):
    any_spec = pl.BlockSpec(memory_space=pl.ANY)
    blocks = (PAIRS, 16, TILE, TILE)
    tall, wide = (Q_DEV, D), (D, Q_DEV)
    square = (D, D)
    shapes = [blocks, blocks, (16, D, TILE), tall, tall, wide, wide]
    return pl.pallas_call(
        partial(halo_kernel, extents),
        name="halo",
        out_shape=[jax.ShapeDtypeStruct(s, BF16) for s in shapes],
        in_specs=[any_spec] * 7,
        out_specs=[any_spec] * 7,
        scratch_shapes=[
            pltpu.VMEM(s, BF16)
            for s in [(4, 4, TILE, D), blocks, blocks, (16, D, TILE), tall, tall,
                      square, square, square, square, tall, tall, wide, wide]
        ]
        + [
            pltpu.SemaphoreType.DMA((8,)),
            pltpu.SemaphoreType.DMA((8,)),
            pltpu.SemaphoreType.DMA((7,)),
            pltpu.SemaphoreType.DMA((13,)),
        ],
        compiler_params=pltpu.CompilerParams(
            collective_id=0, has_side_effects=True, vmem_limit_bytes=VMEM_BYTES
        ),
    )(anchors, qf, do, wq, wk, wv, wo)


def attention_kernel(
    lists, counts, kw, vw, q_ref, dp_ref, dpt_ref,
    pk_out, pv_out, att_out, dq_out, dk, dv,
):
    dk[...] = jnp.zeros_like(dk)
    dv[...] = jnp.zeros_like(dv)
    lane = lax.broadcasted_iota(jnp.int32, (TILE, TILE), 1)
    first = lane < HEAD_DIM
    for b in range(4):
        tiles = [lists[b * KT + s] for s in range(KT)]
        count = counts[b]
        at = slice(b * TILE, (b + 1) * TILE)
        q = q_ref[at, :]
        do = dp_ref[at, :]
        zero = jnp.zeros_like(q)
        q2 = jnp.concatenate([jnp.where(first, q, zero), jnp.where(first, zero, q)], axis=0)
        do2 = jnp.concatenate([jnp.where(first, do, zero), jnp.where(first, zero, do)], axis=0)
        keys = jnp.concatenate([kw[0, t] for t in tiles], axis=0)
        values = jnp.concatenate([vw[0, t] for t in tiles], axis=0)
        scores = nt(keys, q2)
        scores = jnp.concatenate(
            [
                scores[s * TILE : (s + 1) * TILE] + jnp.where(s < count, 0.0, NEG).astype(F32)
                for s in range(KT)
            ],
            axis=0,
        )
        top = jnp.max(scores, axis=0, keepdims=True)
        expo = jnp.exp(scores - top)
        prob = expo * (1.0 / jnp.sum(expo, axis=0, keepdims=True))
        half = prob.astype(BF16)
        att2 = tn(values, half)
        att = jnp.concatenate(
            [att2[:HEAD_DIM, :TILE], att2[HEAD_DIM:, TILE:]], axis=0
        ).astype(BF16)
        att_out[:, at] = att
        both = att.astype(F32) * dpt_ref[:, at].astype(F32)
        delta = jnp.concatenate(
            [
                jnp.sum(both[:HEAD_DIM], axis=0, keepdims=True),
                jnp.sum(both[HEAD_DIM:], axis=0, keepdims=True),
            ],
            axis=1,
        )
        dprob = nt(values, do2)
        dscore = (prob * (dprob - delta)).astype(BF16)
        dq2 = tn(keys, dscore)
        dq = jnp.concatenate([dq2[:HEAD_DIM, :TILE], dq2[HEAD_DIM:, TILE:]], axis=0) * SCALE
        dq_out[at, :] = dq.T.astype(BF16)
        dkey = nn(dscore, q2)
        dvalue = nn(half, do2)
        for s in range(KT):
            dk[tiles[s]] += dkey[s * TILE : (s + 1) * TILE]
            dv[tiles[s]] += dvalue[s * TILE : (s + 1) * TILE]
    pk_out[0] = dk[...].astype(BF16)
    pv_out[0] = dv[...].astype(BF16)


def attention(lists, counts, kw, vw, q, dp, dpt):
    blocks = (PAIRS, 16, TILE, TILE)
    by_pair = pl.BlockSpec((1, 16, TILE, TILE), lambda h, *_: (h, 0, 0, 0))
    tall = pl.BlockSpec((Q_DEV, TILE), lambda h, *_: (0, h))
    wide = pl.BlockSpec((TILE, Q_DEV), lambda h, *_: (h, 0))
    return pl.pallas_call(
        attention_kernel,
        name="attention",
        out_shape=[
            jax.ShapeDtypeStruct(blocks, BF16),
            jax.ShapeDtypeStruct(blocks, BF16),
            jax.ShapeDtypeStruct((D, Q_DEV), BF16),
            jax.ShapeDtypeStruct((Q_DEV, D), BF16),
        ],
        grid_spec=pltpu.PrefetchScalarGridSpec(
            num_scalar_prefetch=2,
            grid=(PAIRS,),
            in_specs=[by_pair, by_pair, tall, tall, wide],
            out_specs=[by_pair, by_pair, wide, tall],
            scratch_shapes=[pltpu.VMEM((16, TILE, TILE), F32), pltpu.VMEM((16, TILE, TILE), F32)],
        ),
        compiler_params=pltpu.CompilerParams(vmem_limit_bytes=VMEM_BYTES),
    )(lists, counts, kw, vw, q, dp, dpt)


def grads_kernel(
    extents,
    pk_in, pv_in, awt_in, qft_in, att_in, dq_in, do_in, wq_in, wk_in, wv_in,
    ag_out, qg_out, wg_out,
    pk, pv, awt, qft, att, dq, do, wq, wk, wv,
    snd, rcv, acc, qg_s, ag_s, wg_s,
    mine, core_s, core_r, term, ya_r, xb_r, ta, tb, xa_r, yb_r, zs, zr, fs, fr,
    load_sem, store_sem, hs_sem, hr_sem, cs_sem, cr_sem,
    yas_sem, yar_sem, xbs_sem, xbr_sem, xas_sem, xar_sem, ybs_sem, ybr_sem,
    zs_sem, zr_sem, f_sem,
):
    gx, gy = lax.axis_index("gx"), lax.axis_index("gy")
    core = lax.rem(gy, 2)
    z = lax.rem(gx, 4) * 2 + gy // 2
    x = lax.rem(gx // 4, 4)
    y = gx // 16

    def device(y, x, z, core):
        return ((y * 4 + x) * 4 + z // 2, lax.rem(z, 2) * 2 + core)

    pairs = [(pk_in, pk), (pv_in, pv), (wk_in, wk), (wv_in, wv), (qft_in, qft), (dq_in, dq),
             (att_in, att), (do_in, do), (awt_in, awt), (wq_in, wq)]
    loads = [pltpu.make_async_copy(s, d, load_sem.at[i]) for i, (s, d) in enumerate(pairs)]
    for load in loads:
        load.start()
    sibling = device(y, x, z, 1 - core)
    around = [((gx + dx, gy + dy), inside((gx + dx, gy + dy), extents)) for dx, dy in DIRS]
    always = gx >= 0
    fixed = [sibling]
    fixed += [device(lax.rem(y + k, 4), x, z, core) for k in (1, 2, 3)]
    fixed += [device(y, lax.rem(x + k, 4), z, core) for k in (1, 2, 3)]
    fixed += [device(y, x, lax.rem(z + k, 8), core) for k in range(1, 8)]
    greet(around + [(where, always) for where in fixed])

    def remote(src, dst, send, recv, where):
        return pltpu.make_async_remote_copy(
            src_ref=src, dst_ref=dst, send_sem=send, recv_sem=recv,
            device_id=where, device_id_type=MESH,
        )

    def returning(i):
        dx, dy = DIRS[i]
        row, col = {-1: 0, 1: 3}.get(dx), {-1: 0, 1: 3}.get(dy)
        if row is None:
            src, dst = snd.at[1:3, col], rcv.at[i]
        elif col is None:
            src, dst = snd.at[row, 1:3], rcv.at[i]
        else:
            src, dst = snd.at[row, col], rcv.at[i, 0]
        return remote(src, dst, hs_sem.at[i], hr_sem.at[i], (gx + dx, gy + dy))

    def terms_of(places, keep):
        def side(blocks):
            return jnp.concatenate(
                [
                    jnp.concatenate([blocks[h, r * 4 + c] for r, c in places], axis=0)
                    for h in range(PAIRS)
                ],
                axis=1,
            )

        left_k, left_v = side(pk), side(pv)

        def step(j, _):
            at = pl.ds(pl.multiple_of(j * 256, 256), 256)
            part = nt(left_k, wk[at, :]) + nt(left_v, wv[at, :])
            for n, (r, c) in enumerate(places):
                piece = part[n * TILE : (n + 1) * TILE]
                if keep:
                    acc[r - 1, c - 1, :, at] = piece
                else:
                    snd[r, c, :, at] = piece.astype(BF16)
            return 0

        lax.fori_loop(0, 3, step, 0)

    def send_back(dirs):
        for dx, dy in dirs:
            @pl.when(inside((gx + dx, gy + dy), extents))
            def _(dx=dx, dy=dy):
                returning(DIRS.index((dx, dy))).start()

    for i in range(4):
        loads[i].wait()
    terms_of([(0, c) for c in range(4)], False)
    send_back([(-1, 0), (-1, -1), (-1, 1)])
    terms_of([(3, c) for c in range(4)], False)
    send_back([(1, 0), (1, -1), (1, 1)])
    terms_of([(1, 0), (2, 0), (1, 3), (2, 3)], False)
    send_back([(0, -1), (0, 1)])

    def weight_halves(m, rows_of, columns_of):
        def step(n, _):
            half = jnp.where(n == 0, 1 - core, core)
            part = nn(rows_of(), columns_of(half))

            @pl.when(n == 0)
            def _():
                core_s[m] = part.astype(BF16)

            @pl.when(n == 1)
            def _():
                mine[m] = part
            return 0

        lax.fori_loop(0, 2, step, 0)
        crossing(m).start()

    def crossing(m):
        return remote(core_s.at[m], core_r.at[m], cs_sem.at[m], cr_sem.at[m], sibling)

    def to_row(m):
        k = lax.rem(m - y + 4, 4)
        slot = lax.rem(3 - k + 4, 4)
        return remote(term.at[m, :, 0], ya_r.at[slot], yas_sem.at[m], yar_sem.at[slot],
                      device(m, x, z, core))

    def to_column(m, k):
        goal = lax.rem(x + k, 4)
        return remote(term.at[m, goal, 1], xb_r.at[3 - k, m], xbs_sem.at[k - 1, m],
                      xbr_sem.at[3 - k, m], device(y, goal, z, core))

    def add_cores(m):
        crossing(m).wait()
        for goal in range(4):
            for part in range(2):
                at = slice(goal * 192 + part * 96, goal * 192 + part * 96 + 96)
                term[m, goal, part] = (mine[m, at] + core_r[m, at].astype(F32)).astype(BF16)

        @pl.when(y != m)
        def _():
            to_row(m).start()

        for k in (2, 1, 3):
            to_column(m, k).start()

    def lanes(ref, half):
        return ref[:, pl.ds(pl.multiple_of(half * HALF, 128), HALF)]

    def stacked(ref, half):
        return jnp.concatenate(
            [ref[half * 3 + i].reshape(16 * TILE, TILE) for i in range(3)], axis=1
        )

    def anchor_rows():
        return jnp.concatenate([awt[t] for t in range(16)], axis=1)

    for i in range(4, 8):
        loads[i].wait()
    weight_halves(0, lambda: qft[...], lambda half: lanes(dq, half))
    weight_halves(3, lambda: att[...], lambda half: lanes(do, half))
    add_cores(0)
    add_cores(3)
    loads[8].wait()
    weight_halves(1, anchor_rows, lambda half: stacked(pk, half))
    weight_halves(2, anchor_rows, lambda half: stacked(pv, half))
    add_cores(1)
    add_cores(2)

    terms_of([(1, 1), (1, 2), (2, 1), (2, 2)], True)
    loads[9].wait()

    def query_grad(j, _):
        at = pl.ds(pl.multiple_of(j * 256, 256), 256)
        qg_s[:, at] = nt(dq[...], wq[at, :]).astype(BF16)
        return 0

    lax.fori_loop(0, 3, query_grad, 0)
    qg_copy = pltpu.make_async_copy(qg_s, qg_out, store_sem.at[0])
    qg_copy.start()

    for slot in range(3):
        remote(term.at[0, :, 0], ya_r.at[slot], yas_sem.at[0], yar_sem.at[slot],
               sibling).wait_recv()
    for goal in range(4):
        total = term[y, goal, 0].astype(F32)
        for slot in range(3):
            total = total + ya_r[slot, goal].astype(F32)
        ta[goal] = total.astype(BF16)

    def to_column_second(k):
        goal = lax.rem(x + k, 4)
        return remote(ta.at[goal], xa_r.at[3 - k], xas_sem.at[k - 1], xar_sem.at[3 - k],
                      device(y, goal, z, core))

    for k in (2, 1, 3):
        to_column_second(k).start()
    for k in (1, 2, 3):
        for m in range(4):
            to_column(m, k).wait_recv()
    for m in range(4):
        total = term[m, x, 1].astype(F32)
        for slot in range(3):
            total = total + xb_r[slot, m].astype(F32)
        tb[m] = total.astype(BF16)

    def to_row_second(k):
        goal = lax.rem(y + k, 4)
        return remote(tb.at[goal], yb_r.at[3 - k], ybs_sem.at[k - 1], ybr_sem.at[3 - k],
                      device(goal, x, z, core))

    for k in (2, 1, 3):
        to_row_second(k).start()

    zs[:, 16:32] = jnp.zeros((8, 16, HALF), BF16)
    for k in (1, 2, 3):
        to_column_second(k).wait_recv()
    total = ta[x].astype(F32)
    for slot in range(3):
        total = total + xa_r[slot].astype(F32)
    for i in range(4):
        zs[i, 0:24] = total[i * 24 : (i + 1) * 24].astype(BF16)
    for k in (1, 2, 3):
        to_row_second(k).wait_recv()
    total = tb[y].astype(F32)
    for slot in range(3):
        total = total + yb_r[slot].astype(F32)
    for i in range(4):
        zs[4 + i, 0:24] = total[i * 24 : (i + 1) * 24].astype(BF16)

    def along(k):
        goal = lax.rem(z + k, 8)
        return remote(zs.at[goal], zr.at[7 - k], zs_sem.at[k - 1], zr_sem.at[7 - k],
                      device(y, x, goal, core))

    for k in (4, 3, 5, 2, 6, 1, 7):
        along(k).start()

    for dx, dy in ((0, -1), (0, 1), (-1, 0), (1, 0), (-1, -1), (-1, 1), (1, -1), (1, 1)):
        i = DIRS.index((dx, dy))

        @pl.when(inside((gx - dx, gy - dy), extents))
        def _(i=i, dx=dx, dy=dy):
            returning(i).wait_recv()
            n = 0
            for r in ROWS[dx]:
                for c in ROWS[dy]:
                    acc[r, c] += rcv[i, n].astype(F32)
                    n += 1

    ag_s[...] = acc[...].astype(BF16)
    ag_copy = pltpu.make_async_copy(ag_s, ag_out, store_sem.at[1])
    ag_copy.start()

    for k in range(1, 8):
        along(k).wait_recv()
    total = zs[z].astype(F32)
    for slot in range(7):
        total = total + zr[slot].astype(F32)
    fs[...] = total[0:24]
    last = remote(fs, fr, f_sem.at[0], f_sem.at[1], sibling)
    last.start()
    last.wait()
    low = core == 0
    held, other = fs[...], fr[...]
    held = jnp.where(low, held[0:12], held[12:24])
    other = jnp.where(low, other[0:12], other[12:24])
    norm = (extents[0] * extents[1] * Q_DEV) ** (-0.5)
    wg_s[:, 0:HALF] = jnp.where(low, held, other) * norm
    wg_s[:, HALF:D] = jnp.where(low, other, held) * norm
    wg_copy = pltpu.make_async_copy(wg_s, wg_out, store_sem.at[2])
    wg_copy.start()

    for i, (dx, dy) in enumerate(DIRS):
        @pl.when(inside((gx + dx, gy + dy), extents))
        def _(i=i):
            returning(i).wait_send()
    for m in range(4):
        @pl.when(y != m)
        def _(m=m):
            to_row(m).wait_send()
        for k in (1, 2, 3):
            to_column(m, k).wait_send()
    for k in (1, 2, 3):
        to_column_second(k).wait_send()
        to_row_second(k).wait_send()
    for k in range(1, 8):
        along(k).wait_send()
    qg_copy.wait()
    ag_copy.wait()
    wg_copy.wait()


def grads(extents, pk, pv, awt, qft, att, dq, do, wq, wk, wv):
    any_spec = pl.BlockSpec(memory_space=pl.ANY)
    blocks = (PAIRS, 16, TILE, TILE)
    tall, wide, square = (Q_DEV, D), (D, Q_DEV), (D, D)
    dma = pltpu.SemaphoreType.DMA
    held = [
        (blocks, BF16), (blocks, BF16), ((16, D, TILE), BF16), (wide, BF16), (wide, BF16),
        (tall, BF16), (tall, BF16), (square, BF16), (square, BF16), (square, BF16),
        ((4, 4, TILE, D), BF16), ((8, 2, TILE, D), BF16), ((2, 2, TILE, D), F32), (tall, BF16),
        ((2, 2, TILE, D), BF16), ((12, D), F32),
        ((4, D, HALF), F32), ((4, D, HALF), BF16), ((4, D, HALF), BF16),
        ((4, 4, 2, 96, HALF), BF16), ((3, 4, 96, HALF), BF16), ((3, 4, 96, HALF), BF16),
        ((4, 96, HALF), BF16), ((4, 96, HALF), BF16), ((3, 96, HALF), BF16),
        ((3, 96, HALF), BF16), ((8, 32, HALF), BF16), ((7, 32, HALF), BF16),
        ((24, HALF), F32), ((24, HALF), F32),
    ]
    sems = [(10,), (3,), (8,), (8,), (4,), (4,), (4,), (3,), (3, 4), (3, 4), (3,), (3,), (3,),
            (3,), (7,), (7,), (2,)]
    return pl.pallas_call(
        partial(grads_kernel, extents),
        name="grads",
        out_shape=[
            jax.ShapeDtypeStruct((2, 2, TILE, D), BF16),
            jax.ShapeDtypeStruct(tall, BF16),
            jax.ShapeDtypeStruct((12, D), F32),
        ],
        in_specs=[any_spec] * 10,
        out_specs=[any_spec] * 3,
        scratch_shapes=[pltpu.VMEM(s, t) for s, t in held] + [dma(s) for s in sems],
        compiler_params=pltpu.CompilerParams(
            collective_id=1, has_side_effects=True, vmem_limit_bytes=VMEM_BYTES
        ),
    )(pk, pv, awt, qft, att, dq, do, wq, wk, wv)


def on_device(
    extents,
    query_feats, anchors, tile_lists, tile_counts, out_grad, w_query, w_key, w_value, w_out,
):
    qf = query_feats.reshape(Q_DEV, D)
    do = out_grad.reshape(Q_DEV, D)
    lists = tile_lists.reshape(-1)
    counts = tile_counts.reshape(-1)
    kw, vw, awt, q, dp, dpt, qft = halo(extents, anchors, qf, do, w_query, w_key, w_value, w_out)
    pk, pv, att, dq = attention(lists, counts, kw, vw, q, dp, dpt)
    anchor_grad, query_grad, weight_grads = grads(
        extents, pk, pv, awt, qft, att, dq, do, w_query, w_key, w_value
    )
    return query_grad.reshape(query_feats.shape), anchor_grad, weight_grads


def solution(mesh):
    four = P("gx", "gy", None, None)
    in_specs = (four, four, four, P("gx", "gy", None), four, P(), P(), P(), P())
    out_specs = (four, four, P(("gx", "gy"), None))
    extents = (mesh.shape["gx"], mesh.shape["gy"])
    return jax.shard_map(
        partial(on_device, extents),
        mesh=mesh, in_specs=in_specs, out_specs=out_specs, check_vma=False,
    )
```

time: 1750 us -> 148 us (0.08)
  blocking collectives: 719 us -> 0 us
  starting transfers between devices: 588 us -> 0 us
  local copies, waits for them, and re-layouts: 219 us -> 6.04 us
  Pallas kernels: 0 us -> 141 us
  waiting for transfers between devices: 84.9 us -> 0 us
  matrix products: 79.4 us -> 0 us
  other arithmetic: 42.7 us -> 0 us
    unnamed x1 -> x0, blocking collectives: 719 us -> none
    unnamed x64 -> x0, starting transfers between devices: 500 us -> none
    pallas_call x0 -> x3, Pallas kernels: none -> 141 us  [the longest x1 72.9 us: grads(): pl.pallas_call(partial(grads_kernel, extents), name='grads', out_shape=[j...]
    unnamed x53 -> x5, local copies, waits for them, and re-layouts: 102 us -> 4.76 us
    ppermute x12 -> x0, starting transfers between devices: 88 us -> none  [the longest x8 75.4 us: from_behind(): return lax.ppermute(shard, axis, pairs)]
    ppermute x12 -> x0, waiting for transfers between devices: 84.7 us -> none  [the longest x8 45.5 us: from_behind(): return lax.ppermute(shard, axis, pairs)]
    dot_general x20 -> x0, matrix products: 70.1 us -> none  [the longest x2 28.5 us: attention_step(): jnp.dot(selector, slot_grads, precision=lax.Precision.HIGHEST, preferred_...]
    reshape x8 -> x1, local copies, waits for them, and re-layouts: 28 us -> 1.27 us  [on_device(): lists = tile_lists.reshape(-1)]
  transfers between devices with their start and end apart: 76 -> 0, of which waited for: 5 -> 0; matrix products, arithmetic and copies ran while one was open for 2% -> 0% of each run, Pallas kernels for 0% -> 0%
where the time goes in v1:
time: 148 us
  Pallas kernels  141 us (95%)
  local copies, waits for them, and re-layouts  6.04 us (4%)
    pallas_call x1, Pallas kernels, grads(): pl.pallas_call(partial(grads_kernel, extents), name='grads', out_shape=[j...  72.9 us
    pallas_call x1, Pallas kernels, halo(): pl.pallas_call(partial(halo_kernel, extents), name='halo', out_shape=[jax...  41.2 us
    pallas_call x1, Pallas kernels, attention(): pl.pallas_call(attention_kernel, name='attention', out_shape=[jax.ShapeDt...  26.9 us
    unnamed x5, local copies, waits for them, and re-layouts  4.76 us

profile of v1, /device:TPU:1, one launch (start us, length us, event | category | flops | bytes accessed | tf_op | source)
XLA Modules:
  0.0 147.7 jit_solution(16108904338053190121)
XLA Ops:
  0.6 1.3 reshape.21.lists
  1.9 41.2 %halo.1 = (bf16[6,16,128,128]{3,2,1,0:T(8,128)(2,1)}, bf16[6,16,128,128]{3,2,1,0:T(8,128)(2,1)}, bf16[16,768,128]{2,1,0:T(8,128)(2,1)}, bf16[512,768]{1,0:T(8,12...) custom-call(bf16[2,2,128,768]{3,2,1,0:T(8,128)(2,1)} %anchors.1, ...), custom_call_target="tpu_custom_call" | custom-call | tf_op jit(solution)/shard_map/halo/pallas_call | solution.py:191
  43.1 26.9 %attention.1 = (bf16[6,16,128,128]{3,2,1,0:T(8,128)(2,1)}, bf16[6,16,128,128]{3,2,1,0:T(8,128)(2,1)}, bf16[768,512]{1,0:T(8,128)(2,1)}, bf16[512,768]{1,0:T(8,128)(2,1)}) custom-call(s32[16]{0:T(128)} %reshape.21.lists, s32[4]{0:T(128)} %bitcast.8, bf16[6,16,128,128]{3,2,1,0:T(8,128)(2,1)} %get-tuple-element.17.kw, ...), custom_call_target="tpu_custom_call" | custom-call | tf_op jit(solution)/shard_map/attention/pallas_call | solution.py:277
  70.0 72.9 %grads.1 = (bf16[2,2,128,768]{3,2,1,0:T(8,128)(2,1)}, bf16[512,768]{1,0:T(8,128)(2,1)}, f32[12,768]{1,0:T(8,128)}) custom-call(bf16[6,16,128,128]{3,2,1,0:T(8,128)(2,1)} %get-tuple-element.22.pk_in, bf16[6,16,128,128]{3,2,1,0:T(8,128)(2,1)} %get-tuple-element.23.pv_in, bf16[16,768,128]{2,1,0:T(8,128)(2,1)} %get-tuple-element.24.awt_in, ...), custom_call_target="tpu_custom_call" | custom-call | tf_op jit(solution)/shard_map/grads/pallas_call | solution.py:598
  142.9 0.0 copy-start
  142.9 2.1 %copy.15 = bf16[1,1,512,768]{3,2,1,0:T(8,128)(2,1)} copy(bf16[1,1,512,768]{3,2,1,0:T(8,128)(2,1)} %bitcast.7) | data formatting | bytes 1572864
  145.0 2.1 %copy.16 = bf16[2,2,128,768]{3,2,1,0:T(8,128)(2,1)} copy(bf16[2,2,128,768]{3,2,1,0:T(8,128)(2,1)} %get-tuple-element.35) | data formatting | bytes 1572864
  147.1 0.0 copy-done
  147.1 0.6 copy.17
Async XLA Ops:
  142.9 4.2 %copy-start = (f32[12,768]{1,0:T(8,128)S(1)}, f32[12,768]{1,0:T(8,128)}, u32[]{:S(2)}) copy-start(f32[12,768]{1,0:T(8,128)} %get-tuple-element.36) | copy-start | bytes 110596

commit v2 on v1

--- a/solution.py
+++ b/solution.py
@@ -23,9 +23,11 @@
 VMEM_BYTES = 56 * 1024 * 1024
 
 DIRS = ((-1, 0), (1, 0), (-1, -1), (-1, 1), (1, -1), (1, 1), (0, -1), (0, 1))
-OWN = {-1: (0, 1), 0: (0, 2), 1: (1, 2)}
-LAND = {-1: (3, 4), 0: (1, 3), 1: (0, 1)}
-ROWS = {-1: (1,), 0: (0, 1), 1: (0,)}
+CENTRE = ((1, 1), (1, 2), (2, 1), (2, 2))
+BESIDE = ((1, 0), (2, 0), (1, 3), (2, 3))
+ENDS = ((0, 1), (0, 2), (3, 1), (3, 2))
+CORNERS = ((0, 0), (0, 3), (3, 0), (3, 3))
+HELD = CENTRE + BESIDE + ENDS + CORNERS
 
 
 def nn(left, right):
@@ -56,12 +58,16 @@
     pl.semaphore_wait(barrier, total)
 
 
+def straight(dx, dy, gy):
+    return ((dx, dy) == (1, -1)) & (gy == 2) | ((dx, dy) == (-1, 1)) & (gy == 1)
+
+
 def halo_kernel(
     extents,
     anchors, qf_in, do_in, wq_in, wk_in, wv_in, wo_in,
     kw_out, vw_out, awt_out, q_out, dp_out, dpt_out, qft_out,
     win, kw, vw, awt, qf, do, wq, wk, wv, wo, q_s, dp_s, dpt_s, qft_s,
-    send_sem, recv_sem, load_sem, store_sem,
+    end_send, end_recv, side_send, side_recv, corner_send, corner_recv, load_sem, store_sem,
 ):
     gx, gy = lax.axis_index("gx"), lax.axis_index("gy")
     loads = [
@@ -76,28 +82,53 @@
     own.start()
     greet([((gx + dx, gy + dy), inside((gx + dx, gy + dy), extents)) for dx, dy in DIRS])
 
-    def sending(i):
-        dx, dy = DIRS[i]
-        (r0, r1), (c0, c1) = OWN[dx], OWN[dy]
-        (p0, p1), (q0, q1) = LAND[dx], LAND[dy]
+    def exists(dx, dy):
+        return inside((gx + dx, gy + dy), extents)
+
+    def remote(src, dst, send, recv, dx, dy):
         return pltpu.make_async_remote_copy(
-            src_ref=anchors.at[r0:r1, c0:c1],
-            dst_ref=win.at[p0:p1, q0:q1],
-            send_sem=send_sem.at[i],
-            recv_sem=recv_sem.at[i],
-            device_id=(gx + dx, gy + dy),
-            device_id_type=MESH,
+            src_ref=src, dst_ref=dst, send_sem=send, recv_sem=recv,
+            device_id=(gx + dx, gy + dy), device_id_type=MESH,
         )
 
-    for i, (dx, dy) in enumerate(DIRS):
-        @pl.when(inside((gx + dx, gy + dy), extents))
-        def _(i=i):
-            sending(i).start()
+    def to_end(dx, c):
+        n, row, goal = (0, 1, 0) if dx == 1 else (1, 0, 3)
+        return remote(anchors.at[row, c], win.at[goal, c + 1], end_send.at[n, c],
+                      end_recv.at[n, c], dx, 0)
+
+    def to_side(dy):
+        n, col, goal = (0, 1, 0) if dy == 1 else (1, 0, 3)
+        return remote(anchors.at[:, col], win.at[1:3, goal], side_send.at[n], side_recv.at[n],
+                      0, dy)
+
+    def to_corner(dx, dy, direct):
+        row, goal_row = (1, 0) if dx == 1 else (0, 3)
+        col, goal_col = (1, 0) if dy == 1 else (0, 3)
+        n, p = int(dx == -1), int(dy == -1)
+        src = anchors.at[row, col] if direct else win.at[goal_row, col + 1]
+        return remote(src, win.at[goal_row, goal_col], corner_send.at[n, p],
+                      corner_recv.at[n, p], dx if direct else 0, dy)
+
+    first = jnp.where(gy < 2, 1, 0)
+    for turn in range(2):
+        for dx in (1, -1):
+            @pl.when(exists(dx, 0))
+            def _(turn=turn, dx=dx):
+                to_end(dx, first if turn == 0 else 1 - first).start()
+    for dx, dy in ((1, -1), (-1, 1)):
+        @pl.when(exists(dx, dy) & straight(dx, dy, gy))
+        def _(dx=dx, dy=dy):
+            to_corner(dx, dy, True).start()
+    for dy in (1, -1):
+        @pl.when(exists(0, dy))
+        def _(dy=dy):
+            to_side(dy).start()
 
     for dx, dy in DIRS:
-        (p0, p1), (q0, q1) = LAND[dx], LAND[dy]
-
-        @pl.when(jnp.logical_not(inside((gx - dx, gy - dy), extents)))
+        p0, p1 = {-1: (3, 4), 0: (1, 3), 1: (0, 1)}[dx]
+        q0, q1 = {-1: (3, 4), 0: (1, 3), 1: (0, 1)}[dy]
+
+        @pl.when(jnp.logical_not(exists(-dx, -dy)))
         def _(p0=p0, p1=p1, q0=q0, q1=q1):
             win[p0:p1, q0:q1] = jnp.zeros((p1 - p0, q1 - q0, TILE, D), BF16)
 
@@ -138,46 +169,68 @@
 
     def project_tiles(places):
         rows = jnp.concatenate([win[r, c] for r, c in places], axis=0)
+        base = HELD.index(places[0])
 
         def step(j, _):
             at = pl.ds(pl.multiple_of(j * 256, 256), 256)
             for weight, goal in ((wk, kw), (wv, vw)):
                 part = nn(rows, weight[:, at]).astype(BF16)
-                for n, (r, c) in enumerate(places):
+                for n in range(4):
                     for i in range(2):
-                        goal[2 * j + i, r * 4 + c] = part[
+                        goal[2 * j + i, base + n] = part[
                             n * TILE : (n + 1) * TILE, i * TILE : (i + 1) * TILE
                         ]
             return 0
 
         lax.fori_loop(0, 3, step, 0)
-        for r, c in places:
-            awt[r * 4 + c] = win[r, c].T
-
-    def arrive(dx, dy):
-        @pl.when(inside((gx - dx, gy - dy), extents))
-        def _():
-            sending(DIRS.index((dx, dy))).wait_recv()
-
-    project_tiles([(1, 1), (1, 2), (2, 1), (2, 2)])
-    arrive(0, 1)
-    project_tiles([(1, 0), (2, 0)])
-    arrive(0, -1)
-    project_tiles([(1, 3), (2, 3)])
-    store(kw.at[:, 4:12], kw_out.at[:, 4:12])
-    store(vw.at[:, 4:12], vw_out.at[:, 4:12])
-    store(awt.at[4:12], awt_out.at[4:12])
-    for dx, first in ((1, 0), (-1, 12)):
-        for dy in (0, -1, 1):
-            arrive(dx, dy)
-        project_tiles([(first // 4, c) for c in range(4)])
-        store(kw.at[:, first : first + 4], kw_out.at[:, first : first + 4])
-        store(vw.at[:, first : first + 4], vw_out.at[:, first : first + 4])
-        store(awt.at[first : first + 4], awt_out.at[first : first + 4])
-    for i, (dx, dy) in enumerate(DIRS):
-        @pl.when(inside((gx + dx, gy + dy), extents))
-        def _(i=i):
-            sending(i).wait_send()
+        for n, (r, c) in enumerate(places):
+            awt[base + n] = win[r, c].T
+        at = slice(base, base + 4)
+        store(kw.at[:, at], kw_out.at[:, at])
+        store(vw.at[:, at], vw_out.at[:, at])
+        store(awt.at[at], awt_out.at[at])
+
+    project_tiles(CENTRE)
+    for dy in (1, -1):
+        @pl.when(exists(0, -dy))
+        def _(dy=dy):
+            to_side(dy).wait_recv()
+    project_tiles(BESIDE)
+    for turn in range(2):
+        for dx in (1, -1):
+            c = first if turn == 0 else 1 - first
+
+            @pl.when(exists(-dx, 0))
+            def _(dx=dx, c=c):
+                to_end(dx, c).wait_recv()
+
+            for dy, col in ((1, 1), (-1, 0)):
+                @pl.when(exists(-dx, 0) & exists(0, dy) & (c == col)
+                         & jnp.logical_not(straight(dx, dy, gy)))
+                def _(dx=dx, dy=dy):
+                    to_corner(dx, dy, False).start()
+    project_tiles(ENDS)
+    for dx in (1, -1):
+        for dy in (1, -1):
+            @pl.when(exists(-dx, -dy))
+            def _(dx=dx, dy=dy):
+                to_corner(dx, dy, True).wait_recv()
+    project_tiles(CORNERS)
+    for dx in (1, -1):
+        @pl.when(exists(dx, 0))
+        def _(dx=dx):
+            to_end(dx, 0).wait_send()
+            to_end(dx, 1).wait_send()
+        for dy in (1, -1):
+            here = straight(dx, dy, gy)
+
+            @pl.when(exists(dx, dy) & here | exists(-dx, dy) & jnp.logical_not(here))
+            def _(dx=dx, dy=dy):
+                to_corner(dx, dy, True).wait_send()
+    for dy in (1, -1):
+        @pl.when(exists(0, dy))
+        def _(dy=dy):
+            to_side(dy).wait_send()
     for copy in stores:
         copy.wait()
 
@@ -200,10 +253,8 @@
                       square, square, square, square, tall, tall, wide, wide]
         ]
         + [
-            pltpu.SemaphoreType.DMA((8,)),
-            pltpu.SemaphoreType.DMA((8,)),
-            pltpu.SemaphoreType.DMA((7,)),
-            pltpu.SemaphoreType.DMA((13,)),
+            pltpu.SemaphoreType.DMA(s)
+            for s in [(2, 2), (2, 2), (2,), (2,), (2, 2), (2, 2), (7,), (16,)]
         ],
         compiler_params=pltpu.CompilerParams(
             collective_id=0, has_side_effects=True, vmem_limit_bytes=VMEM_BYTES
@@ -212,7 +263,7 @@
 
 
 def attention_kernel(
-    lists, counts, kw, vw, q_ref, dp_ref, dpt_ref,
+    lists, counts, order, kw, vw, q_ref, dp_ref, dpt_ref,
     pk_out, pv_out, att_out, dq_out, dk, dv,
 ):
     dk[...] = jnp.zeros_like(dk)
@@ -220,8 +271,8 @@
     lane = lax.broadcasted_iota(jnp.int32, (TILE, TILE), 1)
     first = lane < HEAD_DIM
     for b in range(4):
-        tiles = [lists[b * KT + s] for s in range(KT)]
-        count = counts[b]
+        tiles = [order[lists[0, 0, b, s]] for s in range(KT)]
+        count = counts[0, 0, b]
         at = slice(b * TILE, (b + 1) * TILE)
         q = q_ref[at, :]
         do = dp_ref[at, :]
@@ -269,7 +320,7 @@
     pv_out[0] = dv[...].astype(BF16)
 
 
-def attention(lists, counts, kw, vw, q, dp, dpt):
+def attention(lists, counts, order, kw, vw, q, dp, dpt):
     blocks = (PAIRS, 16, TILE, TILE)
     by_pair = pl.BlockSpec((1, 16, TILE, TILE), lambda h, *_: (h, 0, 0, 0))
     tall = pl.BlockSpec((Q_DEV, TILE), lambda h, *_: (0, h))
@@ -284,14 +335,14 @@
             jax.ShapeDtypeStruct((Q_DEV, D), BF16),
         ],
         grid_spec=pltpu.PrefetchScalarGridSpec(
-            num_scalar_prefetch=2,
+            num_scalar_prefetch=3,
             grid=(PAIRS,),
             in_specs=[by_pair, by_pair, tall, tall, wide],
             out_specs=[by_pair, by_pair, wide, tall],
             scratch_shapes=[pltpu.VMEM((16, TILE, TILE), F32), pltpu.VMEM((16, TILE, TILE), F32)],
         ),
         compiler_params=pltpu.CompilerParams(vmem_limit_bytes=VMEM_BYTES),
-    )(lists, counts, kw, vw, q, dp, dpt)
+    )(lists, counts, order, kw, vw, q, dp, dpt)
 
 
 def grads_kernel(
@@ -299,10 +350,11 @@
     pk_in, pv_in, awt_in, qft_in, att_in, dq_in, do_in, wq_in, wk_in, wv_in,
     ag_out, qg_out, wg_out,
     pk, pv, awt, qft, att, dq, do, wq, wk, wv,
-    snd, rcv, acc, qg_s, ag_s, wg_s,
-    mine, core_s, core_r, term, ya_r, xb_r, ta, tb, xa_r, yb_r, zs, zr, fs, fr,
-    load_sem, store_sem, hs_sem, hr_sem, cs_sem, cr_sem,
-    yas_sem, yar_sem, xbs_sem, xbr_sem, xas_sem, xar_sem, ybs_sem, ybr_sem,
+    corner, passed, ends, end_s, end_r, side_s, side_r, corner_r, acc, qg_s, ag_s, wg_s,
+    mine, core_s, core_r, term, yf, yrl, ysum, xf, xrl, xsum,
+    ta, tb, xa_r, yb_r, zs, zr, fs, fr,
+    load_sem, store_sem, pass_send, pass_recv, end_send, end_recv, side_send, side_recv,
+    cs_sem, cr_sem, ys_sem, yr_sem, xs_sem, xr_sem, xas_sem, xar_sem, ybs_sem, ybr_sem,
     zs_sem, zr_sem, f_sem,
 ):
     gx, gy = lax.axis_index("gx"), lax.axis_index("gy")
@@ -314,19 +366,24 @@
     def device(y, x, z, core):
         return ((y * 4 + x) * 4 + z // 2, lax.rem(z, 2) * 2 + core)
 
-    pairs = [(pk_in, pk), (pv_in, pv), (wk_in, wk), (wv_in, wv), (qft_in, qft), (dq_in, dq),
-             (att_in, att), (do_in, do), (awt_in, awt), (wq_in, wq)]
+    def exists(dx, dy):
+        return inside((gx + dx, gy + dy), extents)
+
+    groups = [slice(12, 16), slice(8, 12), slice(4, 8), slice(0, 4)]
+    pairs = [(wk_in, wk), (wv_in, wv)]
+    for at in groups:
+        pairs += [(pk_in.at[:, at], pk.at[:, at]), (pv_in.at[:, at], pv.at[:, at])]
+    pairs += [(qft_in, qft), (dq_in, dq), (att_in, att), (do_in, do), (awt_in, awt), (wq_in, wq)]
     loads = [pltpu.make_async_copy(s, d, load_sem.at[i]) for i, (s, d) in enumerate(pairs)]
     for load in loads:
         load.start()
     sibling = device(y, x, z, 1 - core)
-    around = [((gx + dx, gy + dy), inside((gx + dx, gy + dy), extents)) for dx, dy in DIRS]
-    always = gx >= 0
     fixed = [sibling]
     fixed += [device(lax.rem(y + k, 4), x, z, core) for k in (1, 2, 3)]
     fixed += [device(y, lax.rem(x + k, 4), z, core) for k in (1, 2, 3)]
     fixed += [device(y, x, lax.rem(z + k, 8), core) for k in range(1, 8)]
-    greet(around + [(where, always) for where in fixed])
+    greet([((gx + dx, gy + dy), exists(dx, dy)) for dx, dy in DIRS]
+          + [(where, gx >= 0) for where in fixed])
 
     def remote(src, dst, send, recv, where):
         return pltpu.make_async_remote_copy(
@@ -334,25 +391,12 @@
             device_id=where, device_id_type=MESH,
         )
 
-    def returning(i):
-        dx, dy = DIRS[i]
-        row, col = {-1: 0, 1: 3}.get(dx), {-1: 0, 1: 3}.get(dy)
-        if row is None:
-            src, dst = snd.at[1:3, col], rcv.at[i]
-        elif col is None:
-            src, dst = snd.at[row, 1:3], rcv.at[i]
-        else:
-            src, dst = snd.at[row, col], rcv.at[i, 0]
-        return remote(src, dst, hs_sem.at[i], hr_sem.at[i], (gx + dx, gy + dy))
-
-    def terms_of(places, keep):
+    def terms_of(group, goal):
+        base = 4 * group
+
         def side(blocks):
             return jnp.concatenate(
-                [
-                    jnp.concatenate([blocks[h, r * 4 + c] for r, c in places], axis=0)
-                    for h in range(PAIRS)
-                ],
-                axis=1,
+                [blocks[h, base : base + 4].reshape(4 * TILE, TILE) for h in range(PAIRS)], axis=1
             )
 
         left_k, left_v = side(pk), side(pv)
@@ -360,30 +404,78 @@
         def step(j, _):
             at = pl.ds(pl.multiple_of(j * 256, 256), 256)
             part = nt(left_k, wk[at, :]) + nt(left_v, wv[at, :])
-            for n, (r, c) in enumerate(places):
-                piece = part[n * TILE : (n + 1) * TILE]
-                if keep:
-                    acc[r - 1, c - 1, :, at] = piece
-                else:
-                    snd[r, c, :, at] = piece.astype(BF16)
+            for n in range(4):
+                goal[n, :, at] = part[n * TILE : (n + 1) * TILE].astype(goal.dtype)
             return 0
 
         lax.fori_loop(0, 3, step, 0)
 
-    def send_back(dirs):
-        for dx, dy in dirs:
-            @pl.when(inside((gx + dx, gy + dy), extents))
-            def _(dx=dx, dy=dy):
-                returning(DIRS.index((dx, dy))).start()
-
-    for i in range(4):
-        loads[i].wait()
-    terms_of([(0, c) for c in range(4)], False)
-    send_back([(-1, 0), (-1, -1), (-1, 1)])
-    terms_of([(3, c) for c in range(4)], False)
-    send_back([(1, 0), (1, -1), (1, 1)])
-    terms_of([(1, 0), (2, 0), (1, 3), (2, 3)], False)
-    send_back([(0, -1), (0, 1)])
+    def from_corner(rx, ry, direct):
+        n, p = int(rx == 1), int(ry == 1)
+        dst = corner_r.at[n] if direct else passed.at[n, 1 - p]
+        return remote(corner.at[2 * n + p], dst, pass_send.at[n, p], pass_recv.at[n, 1 - p],
+                      (gx + (rx if direct else 0), gy + ry))
+
+    def from_end(rx, c):
+        n = int(rx == 1)
+        return remote(end_s.at[2 * n + c], end_r.at[n, c], end_send.at[n, c], end_recv.at[n, c],
+                      (gx + rx, gy))
+
+    def from_side(ry):
+        p = int(ry == 1)
+        return remote(side_s.at[2 * p : 2 * p + 2], side_r.at[p], side_send.at[p],
+                      side_recv.at[p], (gx, gy + ry))
+
+    for load in loads[0:4]:
+        load.wait()
+    terms_of(3, corner)
+    for rx, ry in ((-1, 1), (1, -1), (-1, -1), (1, 1)):
+        direct = straight(-rx, -ry, gy + ry)
+
+        @pl.when(exists(rx, ry) & direct)
+        def _(rx=rx, ry=ry):
+            from_corner(rx, ry, True).start()
+
+        @pl.when(exists(rx, ry) & jnp.logical_not(direct))
+        def _(rx=rx, ry=ry):
+            from_corner(rx, ry, False).start()
+    for load in loads[4:6]:
+        load.wait()
+    terms_of(2, ends)
+    for load in loads[6:8]:
+        load.wait()
+    terms_of(1, side_s)
+    first = jnp.where(gy < 2, 0, 1)
+    for turn in range(2):
+        c = first if turn == 0 else 1 - first
+        for rx in (-1, 1):
+            n = int(rx == 1)
+            waits = jnp.where(
+                c == 0,
+                exists(rx, -1) & jnp.logical_not(straight(-rx, -1, gy)),
+                exists(rx, 1) & jnp.logical_not(straight(-rx, 1, gy)),
+            )
+
+            @pl.when(exists(rx, 0) & waits)
+            def _(rx=rx, n=n, c=c):
+                remote(corner.at[0], passed.at[n, c], pass_send.at[0, 0], pass_recv.at[n, c],
+                       sibling).wait_recv()
+                end_s[2 * n + c] = (ends[2 * n + c] + passed[n, c].astype(F32)).astype(BF16)
+
+            @pl.when(exists(rx, 0) & jnp.logical_not(waits))
+            def _(n=n, c=c):
+                end_s[2 * n + c] = ends[2 * n + c].astype(BF16)
+
+            @pl.when(exists(rx, 0))
+            def _(rx=rx, c=c):
+                from_end(rx, c).start()
+    for ry in (-1, 1):
+        @pl.when(exists(0, ry))
+        def _(ry=ry):
+            from_side(ry).start()
+
+    def crossing(m):
+        return remote(core_s.at[m], core_r.at[m], cs_sem.at[m], cr_sem.at[m], sibling)
 
     def weight_halves(m, rows_of, columns_of):
         def step(n, _):
@@ -393,6 +485,7 @@
             @pl.when(n == 0)
             def _():
                 core_s[m] = part.astype(BF16)
+                crossing(m).start()
 
             @pl.when(n == 1)
             def _():
@@ -400,21 +493,37 @@
             return 0
 
         lax.fori_loop(0, 2, step, 0)
-        crossing(m).start()
-
-    def crossing(m):
-        return remote(core_s.at[m], core_r.at[m], cs_sem.at[m], cr_sem.at[m], sibling)
-
-    def to_row(m):
-        k = lax.rem(m - y + 4, 4)
-        slot = lax.rem(3 - k + 4, 4)
-        return remote(term.at[m, :, 0], ya_r.at[slot], yas_sem.at[m], yar_sem.at[slot],
-                      device(m, x, z, core))
-
-    def to_column(m, k):
-        goal = lax.rem(x + k, 4)
-        return remote(term.at[m, goal, 1], xb_r.at[3 - k, m], xbs_sem.at[k - 1, m],
-                      xbr_sem.at[3 - k, m], device(y, goal, z, core))
+
+    y_up, y_down = device(lax.rem(y + 1, 4), x, z, core), device(lax.rem(y + 3, 4), x, z, core)
+    x_next, x_over, x_last = lax.rem(x + 1, 4), lax.rem(x + 2, 4), lax.rem(x + 3, 4)
+    x_up, x_down = device(y, x_next, z, core), device(y, x_last, z, core)
+
+    def y_copy(m, i):
+        low, high = slice(0, 2), slice(2, 4)
+        src, dst, where = [
+            (term.at[m, high, 0], yf.at[0, high], y_up),
+            (term.at[m, low, 0], yf.at[1, low], y_down),
+            (term.at[m, low, 0], yrl.at[0], y_up),
+            (term.at[m, high, 0], yrl.at[1], y_down),
+            (ysum.at[0], yf.at[0, low], y_up),
+            (ysum.at[1], yf.at[1, high], y_down),
+        ][i]
+        return remote(src, dst, ys_sem.at[i], yr_sem.at[i], where)
+
+    def x_copy(m, i):
+        low, high = slice(0, 48), slice(48, 96)
+        src, dst, where = [
+            (term.at[m, x_next, 1, high], xf.at[m, 0, high], x_up),
+            (term.at[m, x_last, 1, low], xf.at[m, 1, low], x_down),
+            (term.at[m, x_over, 1, low], xrl.at[m, 0], x_up),
+            (term.at[m, x_over, 1, high], xrl.at[m, 1], x_down),
+            (xsum.at[m, 0], xf.at[m, 0, low], x_up),
+            (xsum.at[m, 1], xf.at[m, 1, high], x_down),
+        ][i]
+        return remote(src, dst, xs_sem.at[m, i], xr_sem.at[m, i], where)
+
+    def y_place(m):
+        return lax.rem(m - y + 4, 4)
 
     def add_cores(m):
         crossing(m).wait()
@@ -423,12 +532,51 @@
                 at = slice(goal * 192 + part * 96, goal * 192 + part * 96 + 96)
                 term[m, goal, part] = (mine[m, at] + core_r[m, at].astype(F32)).astype(BF16)
 
-        @pl.when(y != m)
+        @pl.when(y_place(m) == 2)
         def _():
-            to_row(m).start()
-
-        for k in (2, 1, 3):
-            to_column(m, k).start()
+            y_copy(m, 2).start()
+            y_copy(m, 3).start()
+
+        for i in (2, 3):
+            x_copy(m, i).start()
+
+        @pl.when(y_place(m) == 1)
+        def _():
+            y_copy(m, 0).start()
+
+        @pl.when(y_place(m) == 3)
+        def _():
+            y_copy(m, 1).start()
+
+        for i in (0, 1):
+            x_copy(m, i).start()
+
+    def hand_on(m):
+        @pl.when(y_place(m) == 1)
+        def _():
+            y_copy(m, 2).wait_recv()
+            for goal in range(2):
+                ysum[0, goal] = (
+                    term[m, goal, 0].astype(F32) + yrl[0, goal].astype(F32)
+                ).astype(BF16)
+            y_copy(m, 4).start()
+
+        @pl.when(y_place(m) == 3)
+        def _():
+            y_copy(m, 3).wait_recv()
+            for goal in range(2):
+                ysum[1, goal] = (
+                    term[m, 2 + goal, 0].astype(F32) + yrl[1, goal].astype(F32)
+                ).astype(BF16)
+            y_copy(m, 5).start()
+
+        for n, goal in ((0, x_next), (1, x_last)):
+            x_copy(m, 2 + n).wait_recv()
+            at = slice(48 * n, 48 * n + 48)
+            xsum[m, n] = (
+                term[m, goal, 1, at].astype(F32) + xrl[m, n].astype(F32)
+            ).astype(BF16)
+            x_copy(m, 4 + n).start()
 
     def lanes(ref, half):
         return ref[:, pl.ds(pl.multiple_of(half * HALF, 128), HALF)]
@@ -441,20 +589,24 @@
     def anchor_rows():
         return jnp.concatenate([awt[t] for t in range(16)], axis=1)
 
-    for i in range(4, 8):
-        loads[i].wait()
+    for load in loads[10:14]:
+        load.wait()
     weight_halves(0, lambda: qft[...], lambda half: lanes(dq, half))
     weight_halves(3, lambda: att[...], lambda half: lanes(do, half))
     add_cores(0)
+    for load in loads[8:10] + loads[14:15]:
+        load.wait()
+    weight_halves(1, anchor_rows, lambda half: stacked(pk, half))
     add_cores(3)
-    loads[8].wait()
-    weight_halves(1, anchor_rows, lambda half: stacked(pk, half))
+    hand_on(0)
     weight_halves(2, anchor_rows, lambda half: stacked(pv, half))
     add_cores(1)
+    hand_on(3)
     add_cores(2)
 
-    terms_of([(1, 1), (1, 2), (2, 1), (2, 2)], True)
-    loads[9].wait()
+    terms_of(0, acc)
+    hand_on(1)
+    loads[15].wait()
 
     def query_grad(j, _):
         at = pl.ds(pl.multiple_of(j * 256, 256), 256)
@@ -464,15 +616,13 @@
     lax.fori_loop(0, 3, query_grad, 0)
     qg_copy = pltpu.make_async_copy(qg_s, qg_out, store_sem.at[0])
     qg_copy.start()
-
-    for slot in range(3):
-        remote(term.at[0, :, 0], ya_r.at[slot], yas_sem.at[0], yar_sem.at[slot],
-               sibling).wait_recv()
+    hand_on(2)
+
+    for i in (0, 1, 4, 5):
+        y_copy(0, i).wait_recv()
     for goal in range(4):
         total = term[y, goal, 0].astype(F32)
-        for slot in range(3):
-            total = total + ya_r[slot, goal].astype(F32)
-        ta[goal] = total.astype(BF16)
+        ta[goal] = (total + yf[0, goal].astype(F32) + yf[1, goal].astype(F32)).astype(BF16)
 
     def to_column_second(k):
         goal = lax.rem(x + k, 4)
@@ -481,14 +631,11 @@
 
     for k in (2, 1, 3):
         to_column_second(k).start()
-    for k in (1, 2, 3):
-        for m in range(4):
-            to_column(m, k).wait_recv()
     for m in range(4):
+        for i in (0, 1, 4, 5):
+            x_copy(m, i).wait_recv()
         total = term[m, x, 1].astype(F32)
-        for slot in range(3):
-            total = total + xb_r[slot, m].astype(F32)
-        tb[m] = total.astype(BF16)
+        tb[m] = (total + xf[m, 0].astype(F32) + xf[m, 1].astype(F32)).astype(BF16)
 
     def to_row_second(k):
         goal = lax.rem(y + k, 4)
@@ -522,17 +669,30 @@
     for k in (4, 3, 5, 2, 6, 1, 7):
         along(k).start()
 
-    for dx, dy in ((0, -1), (0, 1), (-1, 0), (1, 0), (-1, -1), (-1, 1), (1, -1), (1, 1)):
-        i = DIRS.index((dx, dy))
-
-        @pl.when(inside((gx - dx, gy - dy), extents))
-        def _(i=i, dx=dx, dy=dy):
-            returning(i).wait_recv()
-            n = 0
-            for r in ROWS[dx]:
-                for c in ROWS[dy]:
-                    acc[r, c] += rcv[i, n].astype(F32)
-                    n += 1
+    for ry in (-1, 1):
+        @pl.when(exists(0, -ry))
+        def _(ry=ry):
+            from_side(ry).wait_recv()
+            p, c = (1, 0) if ry == 1 else (0, 1)
+            for r in range(2):
+                acc[2 * r + c] += side_r[p, r].astype(F32)
+    for rx in (-1, 1):
+        n, r = (1, 0) if rx == 1 else (0, 1)
+
+        @pl.when(exists(-rx, 0))
+        def _(rx=rx, n=n, r=r):
+            for c in range(2):
+                from_end(rx, c).wait_recv()
+                acc[2 * r + c] += end_r[n, c].astype(F32)
+    for rx, ry in ((-1, 1), (1, -1)):
+        n, r = (1, 0) if rx == 1 else (0, 1)
+        p, c = (1, 0) if ry == 1 else (0, 1)
+
+        @pl.when(exists(-rx, -ry) & straight(-rx, -ry, gy))
+        def _(rx=rx, ry=ry, n=n, p=p, r=r, c=c):
+            remote(corner.at[0], corner_r.at[n], pass_send.at[0, 0], pass_recv.at[n, 1 - p],
+                   sibling).wait_recv()
+            acc[2 * r + c] += corner_r[n].astype(F32)
 
     ag_s[...] = acc[...].astype(BF16)
     ag_copy = pltpu.make_async_copy(ag_s, ag_out, store_sem.at[1])
@@ -557,16 +717,24 @@
     wg_copy = pltpu.make_async_copy(wg_s, wg_out, store_sem.at[2])
     wg_copy.start()
 
-    for i, (dx, dy) in enumerate(DIRS):
-        @pl.when(inside((gx + dx, gy + dy), extents))
-        def _(i=i):
-            returning(i).wait_send()
+    for rx in (-1, 1):
+        @pl.when(exists(rx, 0))
+        def _(rx=rx):
+            from_end(rx, 0).wait_send()
+            from_end(rx, 1).wait_send()
+        for ry in (-1, 1):
+            @pl.when(exists(rx, ry))
+            def _(rx=rx, ry=ry):
+                from_corner(rx, ry, False).wait_send()
+    for ry in (-1, 1):
+        @pl.when(exists(0, ry))
+        def _(ry=ry):
+            from_side(ry).wait_send()
+    for i in range(6):
+        y_copy(0, i).wait_send()
     for m in range(4):
-        @pl.when(y != m)
-        def _(m=m):
-            to_row(m).wait_send()
-        for k in (1, 2, 3):
-            to_column(m, k).wait_send()
+        for i in range(6):
+            x_copy(m, i).wait_send()
     for k in (1, 2, 3):
         to_column_second(k).wait_send()
         to_row_second(k).wait_send()
@@ -581,25 +749,29 @@
     any_spec = pl.BlockSpec(memory_space=pl.ANY)
     blocks = (PAIRS, 16, TILE, TILE)
     tall, wide, square = (Q_DEV, D), (D, Q_DEV), (D, D)
+    four, two = (4, TILE, D), (2, 2, TILE, D)
     dma = pltpu.SemaphoreType.DMA
     held = [
         (blocks, BF16), (blocks, BF16), ((16, D, TILE), BF16), (wide, BF16), (wide, BF16),
         (tall, BF16), (tall, BF16), (square, BF16), (square, BF16), (square, BF16),
-        ((4, 4, TILE, D), BF16), ((8, 2, TILE, D), BF16), ((2, 2, TILE, D), F32), (tall, BF16),
-        ((2, 2, TILE, D), BF16), ((12, D), F32),
+        (four, BF16), (two, BF16), (four, F32), (four, BF16), (two, BF16), (four, BF16),
+        (two, BF16), ((2, TILE, D), BF16), (four, F32), (tall, BF16), (four, BF16),
+        ((12, D), F32),
         ((4, D, HALF), F32), ((4, D, HALF), BF16), ((4, D, HALF), BF16),
-        ((4, 4, 2, 96, HALF), BF16), ((3, 4, 96, HALF), BF16), ((3, 4, 96, HALF), BF16),
+        ((4, 4, 2, 96, HALF), BF16),
+        ((2, 4, 96, HALF), BF16), ((2, 2, 96, HALF), BF16), ((2, 2, 96, HALF), BF16),
+        ((4, 2, 96, HALF), BF16), ((4, 2, 48, HALF), BF16), ((4, 2, 48, HALF), BF16),
         ((4, 96, HALF), BF16), ((4, 96, HALF), BF16), ((3, 96, HALF), BF16),
         ((3, 96, HALF), BF16), ((8, 32, HALF), BF16), ((7, 32, HALF), BF16),
         ((24, HALF), F32), ((24, HALF), F32),
     ]
-    sems = [(10,), (3,), (8,), (8,), (4,), (4,), (4,), (3,), (3, 4), (3, 4), (3,), (3,), (3,),
-            (3,), (7,), (7,), (2,)]
-    return pl.pallas_call(
+    sems = [(16,), (3,), (2, 2), (2, 2), (2, 2), (2, 2), (2,), (2,), (4,), (4,), (6,), (6,),
+            (4, 6), (4, 6), (3,), (3,), (3,), (3,), (7,), (7,), (2,)]
+    anchor_grad, query_grad, weight_grads = pl.pallas_call(
         partial(grads_kernel, extents),
         name="grads",
         out_shape=[
-            jax.ShapeDtypeStruct((2, 2, TILE, D), BF16),
+            jax.ShapeDtypeStruct(four, BF16),
             jax.ShapeDtypeStruct(tall, BF16),
             jax.ShapeDtypeStruct((12, D), F32),
         ],
@@ -610,6 +782,7 @@
             collective_id=1, has_side_effects=True, vmem_limit_bytes=VMEM_BYTES
         ),
     )(pk, pv, awt, qft, att, dq, do, wq, wk, wv)
+    return anchor_grad.reshape(2, 2, TILE, D), query_grad, weight_grads
 
 
 def on_device(
@@ -618,10 +791,9 @@
 ):
     qf = query_feats.reshape(Q_DEV, D)
     do = out_grad.reshape(Q_DEV, D)
-    lists = tile_lists.reshape(-1)
-    counts = tile_counts.reshape(-1)
+    order = jnp.array([HELD.index((w // 4, w % 4)) for w in range(16)], jnp.int32)
     kw, vw, awt, q, dp, dpt, qft = halo(extents, anchors, qf, do, w_query, w_key, w_value, w_out)
-    pk, pv, att, dq = attention(lists, counts, kw, vw, q, dp, dpt)
+    pk, pv, att, dq = attention(tile_lists, tile_counts, order, kw, vw, q, dp, dpt)
     anchor_grad, query_grad, weight_grads = grads(
         extents, pk, pv, awt, qft, att, dq, do, w_query, w_key, w_value
     )

time: 148 us -> 128 us (0.86)
  Pallas kernels: 141 us -> 122 us
    pallas_call x1, Pallas kernels: 72.9 us -> 56.8 us  [grads(): pl.pallas_call(partial(grads_kernel, extents), name='grads', out_shape=[j...]
    pallas_call x1, Pallas kernels: 41.2 us -> 38.5 us  [halo(): pl.pallas_call(partial(halo_kernel, extents), name='halo', out_shape=[jax...]
where the time goes in v2:
time: 128 us
  Pallas kernels  122 us (95%)
  local copies, waits for them, and re-layouts  4.76 us (4%)
    pallas_call x1, Pallas kernels, grads(): pl.pallas_call(partial(grads_kernel, extents), name='grads', out_shape=[j...  56.8 us
    pallas_call x1, Pallas kernels, halo(): pl.pallas_call(partial(halo_kernel, extents), name='halo', out_shape=[jax...  38.5 us
    pallas_call x1, Pallas kernels, attention(): pl.pallas_call(attention_kernel, name='attention', out_shape=[jax.ShapeDt...  27 us
    unnamed x5, local copies, waits for them, and re-layouts  4.76 us

profile of v2, /device:TPU:1, one launch (start us, length us, event | category | flops | bytes accessed | tf_op | source)
XLA Modules:
  0.0 127.6 jit_solution(9916849411819396612)
XLA Ops:
  0.6 38.5 %halo.1 = (bf16[6,16,128,128]{3,2,1,0:T(8,128)(2,1)}, bf16[6,16,128,128]{3,2,1,0:T(8,128)(2,1)}, bf16[16,768,128]{2,1,0:T(8,128)(2,1)}, bf16[512,768]{1,0:T(8,12...) custom-call(bf16[2,2,128,768]{3,2,1,0:T(8,128)(2,1)} %anchors.1, ...), custom_call_target="tpu_custom_call" | custom-call | tf_op jit(solution)/shard_map/halo/pallas_call | solution.py:244
  39.1 27.0 %attention.1 = (bf16[6,16,128,128]{3,2,1,0:T(8,128)(2,1)}, bf16[6,16,128,128]{3,2,1,0:T(8,128)(2,1)}, bf16[768,512]{1,0:T(8,128)(2,1)}, bf16[512,768]{1,0:T(8,128)(2,1)}) custom-call(s32[1,1,4,4]{3,2,1,0:T(4,128)} %lists.1, s32[1,1,4]{2,1,0:T(1,128)} %counts.1, s32[16]{0:T(128)} %constant.2.clone.order, bf16[6,16,128,128]{3,2,1,0:T(8,128)(2,1)} %get-tuple-element.17.kw, ...), custom_call_target="tpu_custom_call" | custom-call | tf_op jit(solution)/shard_map/attention/pallas_call | solution.py:328
  66.1 56.8 %grads.1 = (bf16[4,128,768]{2,1,0:T(8,128)(2,1)}, bf16[512,768]{1,0:T(8,128)(2,1)}, f32[12,768]{1,0:T(8,128)}) custom-call(bf16[6,16,128,128]{3,2,1,0:T(8,128)(2,1)} %get-tuple-element.22.pk_in, bf16[6,16,128,128]{3,2,1,0:T(8,128)(2,1)} %get-tuple-element.23.pv_in, bf16[16,768,128]{2,1,0:T(8,128)(2,1)} %get-tuple-element.24.awt_in, ...), custom_call_target="tpu_custom_call" | custom-call | tf_op jit(solution)/shard_map/grads/pallas_call | solution.py:770
  122.9 0.0 copy-start
  122.9 2.1 %copy.16 = bf16[1,1,512,768]{3,2,1,0:T(8,128)(2,1)} copy(bf16[1,1,512,768]{3,2,1,0:T(8,128)(2,1)} %bitcast.8) | data formatting | bytes 1572864
  124.9 2.1 %copy.17 = bf16[2,2,128,768]{3,2,1,0:T(8,128)(2,1)} copy(bf16[2,2,128,768]{3,2,1,0:T(8,128)(2,1)} %bitcast.7) | data formatting | bytes 1572864
  127.0 0.0 copy-done
  127.0 0.6 copy.18
Async XLA Ops:
  122.9 4.2 %copy-start = (f32[12,768]{1,0:T(8,128)S(1)}, f32[12,768]{1,0:T(8,128)}, u32[]{:S(2)}) copy-start(f32[12,768]{1,0:T(8,128)} %get-tuple-element.36) | copy-start | bytes 110596

commit v3 on v2

--- a/solution.py
+++ b/solution.py
@@ -16,17 +16,23 @@
 Q_DEV = 512
 SCALE = HEAD_DIM ** (-0.5)
 HALF = 384
-NEG = -1e30
+LOG2E = 1.4426950408889634
+DEAD = 1e30
+ORDER = (
+    "X", "C", "A0", "B0", "A1", "B1", "E", "A2", "B2", "A3", "B3", "G", "H0", "H1", "S", "H2", "H3",
+    "K",
+)
 MESH = pl.DeviceIdType.MESH
 F32 = jnp.float32
 BF16 = jnp.bfloat16
+PIECES = ("q", "0", "1", "2", "o", "")
 VMEM_BYTES = 56 * 1024 * 1024
 
 DIRS = ((-1, 0), (1, 0), (-1, -1), (-1, 1), (1, -1), (1, 1), (0, -1), (0, 1))
 CENTRE = ((1, 1), (1, 2), (2, 1), (2, 2))
 BESIDE = ((1, 0), (2, 0), (1, 3), (2, 3))
 ENDS = ((0, 1), (0, 2), (3, 1), (3, 2))
-CORNERS = ((0, 0), (0, 3), (3, 0), (3, 3))
+CORNERS = ((0, 0), (3, 0), (0, 3), (3, 3))
 HELD = CENTRE + BESIDE + ENDS + CORNERS
 
 
@@ -167,15 +173,15 @@
     loads[5].wait()
     own.wait()
 
-    def project_tiles(places):
+    def project_tiles(places, base):
         rows = jnp.concatenate([win[r, c] for r, c in places], axis=0)
-        base = HELD.index(places[0])
+        count = len(places)
 
         def step(j, _):
             at = pl.ds(pl.multiple_of(j * 256, 256), 256)
             for weight, goal in ((wk, kw), (wv, vw)):
                 part = nn(rows, weight[:, at]).astype(BF16)
-                for n in range(4):
+                for n in range(count):
                     for i in range(2):
                         goal[2 * j + i, base + n] = part[
                             n * TILE : (n + 1) * TILE, i * TILE : (i + 1) * TILE
@@ -184,18 +190,19 @@
 
         lax.fori_loop(0, 3, step, 0)
         for n, (r, c) in enumerate(places):
-            awt[base + n] = win[r, c].T
-        at = slice(base, base + 4)
+            awt[:, pl.ds(pl.multiple_of((base + n) * TILE, TILE), TILE)] = win[r, c].T
+        at = pl.ds(base, count)
+        wide = pl.ds(pl.multiple_of(base * TILE, TILE), count * TILE)
         store(kw.at[:, at], kw_out.at[:, at])
         store(vw.at[:, at], vw_out.at[:, at])
-        store(awt.at[at], awt_out.at[at])
-
-    project_tiles(CENTRE)
+        store(awt.at[:, wide], awt_out.at[:, wide])
+
+    project_tiles(CENTRE, 0)
     for dy in (1, -1):
         @pl.when(exists(0, -dy))
         def _(dy=dy):
             to_side(dy).wait_recv()
-    project_tiles(BESIDE)
+    project_tiles(BESIDE, 4)
     for turn in range(2):
         for dx in (1, -1):
             c = first if turn == 0 else 1 - first
@@ -209,13 +216,15 @@
                          & jnp.logical_not(straight(dx, dy, gy)))
                 def _(dx=dx, dy=dy):
                     to_corner(dx, dy, False).start()
-    project_tiles(ENDS)
-    for dx in (1, -1):
-        for dy in (1, -1):
-            @pl.when(exists(-dx, -dy))
-            def _(dx=dx, dy=dy):
-                to_corner(dx, dy, True).wait_recv()
-    project_tiles(CORNERS)
+    project_tiles(ENDS, 8)
+    for turn in range(2):
+        side = lax.rem(gy + 1 + turn, 2)
+        for dy, p in ((1, 0), (-1, 1)):
+            for dx in (1, -1):
+                @pl.when(exists(-dx, -dy) & (side == p))
+                def _(dx=dx, dy=dy):
+                    to_corner(dx, dy, True).wait_recv()
+        project_tiles([(0, 3 * side), (3, 3 * side)], 12 + 2 * side)
     for dx in (1, -1):
         @pl.when(exists(dx, 0))
         def _(dx=dx):
@@ -240,7 +249,7 @@
     blocks = (PAIRS, 16, TILE, TILE)
     tall, wide = (Q_DEV, D), (D, Q_DEV)
     square = (D, D)
-    shapes = [blocks, blocks, (16, D, TILE), tall, tall, wide, wide]
+    shapes = [blocks, blocks, (D, 16 * TILE), tall, tall, wide, wide]
     return pl.pallas_call(
         partial(halo_kernel, extents),
         name="halo",
@@ -249,12 +258,12 @@
         out_specs=[any_spec] * 7,
         scratch_shapes=[
             pltpu.VMEM(s, BF16)
-            for s in [(4, 4, TILE, D), blocks, blocks, (16, D, TILE), tall, tall,
+            for s in [(4, 4, TILE, D), blocks, blocks, (D, 16 * TILE), tall, tall,
                       square, square, square, square, tall, tall, wide, wide]
         ]
         + [
             pltpu.SemaphoreType.DMA(s)
-            for s in [(2, 2), (2, 2), (2,), (2,), (2, 2), (2, 2), (7,), (16,)]
+            for s in [(2, 2), (2, 2), (2,), (2,), (2, 2), (2, 2), (7,), (19,)]
         ],
         compiler_params=pltpu.CompilerParams(
             collective_id=0, has_side_effects=True, vmem_limit_bytes=VMEM_BYTES
@@ -263,41 +272,76 @@
 
 
 def attention_kernel(
-    lists, counts, order, kw, vw, q_ref, dp_ref, dpt_ref,
-    pk_out, pv_out, att_out, dq_out, dk, dv,
+    lists, counts, order, kw, vw, q_ref, dp_ref, dpt_ref, awt_in, qft_in, do_in, wq_in,
+    pk_out, pv_out, w_out, wo_out, qg_out,
+    dk, dv, kv, att_s, dq_s, awt, qft, do_s, wq, sem,
 ):
-    dk[...] = jnp.zeros_like(dk)
-    dv[...] = jnp.zeros_like(dv)
-    lane = lax.broadcasted_iota(jnp.int32, (TILE, TILE), 1)
-    first = lane < HEAD_DIM
-    for b in range(4):
+    pair = pl.program_id(0)
+    loads = [
+        pltpu.make_async_copy(src, dst, sem.at[i])
+        for i, (src, dst) in enumerate([(qft_in, qft), (do_in, do_s), (awt_in, awt), (wq_in, wq)])
+    ]
+
+    @pl.when(pair == 0)
+    def _():
+        for load in loads:
+            load.start()
+
+    slot, last = lax.rem(pair, 2), lax.rem(pair + 1, 2)
+
+    def kept(which):
+        return pl.ds(pl.multiple_of(which * TILE, TILE), TILE)
+
+    before = kept(jnp.maximum(pair - 1, 0))
+
+    def pair_weights(i):
+        at = slice(i * 256, (i + 1) * 256)
+        both = nn(awt[at, :], kv[last]).astype(BF16)
+        w_out[0, 1, at, :] = both[:, :TILE]
+        w_out[0, 2, at, :] = both[:, TILE:]
+
+    def query_weights():
+        w_out[0, 0] = nn(qft[...], dq_s[:, before]).astype(BF16)
+
+    def out_weights():
+        wo_out[...] = nn(att_s[last], do_s[...]).astype(BF16)
+
+    first = lax.broadcasted_iota(jnp.int32, (TILE, TILE), 1) < HEAD_DIM
+
+    def products(b):
         tiles = [order[lists[0, 0, b, s]] for s in range(KT)]
-        count = counts[0, 0, b]
         at = slice(b * TILE, (b + 1) * TILE)
-        q = q_ref[at, :]
-        do = dp_ref[at, :]
+        q, do = q_ref[at, :], dp_ref[at, :]
         zero = jnp.zeros_like(q)
         q2 = jnp.concatenate([jnp.where(first, q, zero), jnp.where(first, zero, q)], axis=0)
         do2 = jnp.concatenate([jnp.where(first, do, zero), jnp.where(first, zero, do)], axis=0)
         keys = jnp.concatenate([kw[0, t] for t in tiles], axis=0)
         values = jnp.concatenate([vw[0, t] for t in tiles], axis=0)
-        scores = nt(keys, q2)
-        scores = jnp.concatenate(
+        return b, at, tiles, q2, do2, keys, values, nt(keys, q2), nt(values, do2)
+
+    def softmax(state):
+        b, at, tiles, q2, do2, keys, values, scores, dprob = state
+        live = [s < counts[0, 0, b] for s in range(KT)]
+        slots = [scores[s * TILE : (s + 1) * TILE] for s in range(KT)]
+        top = jnp.max(slots[0], axis=0, keepdims=True)
+        for s in range(1, KT):
+            best = jnp.max(slots[s], axis=0, keepdims=True)
+            top = jnp.maximum(top, jnp.where(live[s], best, -jnp.inf))
+        top = top * LOG2E
+        expo = jnp.concatenate(
             [
-                scores[s * TILE : (s + 1) * TILE] + jnp.where(s < count, 0.0, NEG).astype(F32)
+                jnp.exp2(slots[s] * LOG2E - (top + jnp.where(live[s], 0.0, DEAD).astype(F32)))
                 for s in range(KT)
             ],
             axis=0,
         )
-        top = jnp.max(scores, axis=0, keepdims=True)
-        expo = jnp.exp(scores - top)
         prob = expo * (1.0 / jnp.sum(expo, axis=0, keepdims=True))
         half = prob.astype(BF16)
         att2 = tn(values, half)
         att = jnp.concatenate(
             [att2[:HEAD_DIM, :TILE], att2[HEAD_DIM:, TILE:]], axis=0
         ).astype(BF16)
-        att_out[:, at] = att
+        att_s[slot, :, at] = att
         both = att.astype(F32) * dpt_ref[:, at].astype(F32)
         delta = jnp.concatenate(
             [
@@ -306,56 +350,118 @@
             ],
             axis=1,
         )
-        dprob = nt(values, do2)
-        dscore = (prob * (dprob - delta)).astype(BF16)
+        return at, tiles, q2, do2, keys, half, (prob * (dprob - delta)).astype(BF16)
+
+    def gradients(state):
+        at, tiles, q2, do2, keys, half, dscore = state
         dq2 = tn(keys, dscore)
         dq = jnp.concatenate([dq2[:HEAD_DIM, :TILE], dq2[HEAD_DIM:, TILE:]], axis=0) * SCALE
-        dq_out[at, :] = dq.T.astype(BF16)
+        dq_s[at, kept(pair)] = dq.T.astype(BF16)
         dkey = nn(dscore, q2)
         dvalue = nn(half, do2)
         for s in range(KT):
             dk[tiles[s]] += dkey[s * TILE : (s + 1) * TILE]
             dv[tiles[s]] += dvalue[s * TILE : (s + 1) * TILE]
-    pk_out[0] = dk[...].astype(BF16)
-    pv_out[0] = dv[...].astype(BF16)
-
-
-def attention(lists, counts, order, kw, vw, q, dp, dpt):
+
+    def all_blocks(weights):
+        dk[...] = jnp.zeros_like(dk)
+        dv[...] = jnp.zeros_like(dv)
+        ahead, behind = {}, {}
+        for turn in range(6):
+            if turn < 4:
+                ahead[turn] = products(turn)
+            if 1 <= turn < 5:
+                behind[turn - 1] = softmax(ahead.pop(turn - 1))
+            if weights:
+                for piece in PIECES[turn].split():
+                    if piece == "q":
+                        query_weights()
+                    elif piece == "o":
+                        out_weights()
+                    else:
+                        pair_weights(int(piece))
+            if turn >= 2:
+                gradients(behind.pop(turn - 2))
+        for t in range(16):
+            key_part, value_part = dk[t].astype(BF16), dv[t].astype(BF16)
+            pk_out[0, t] = key_part
+            pv_out[0, t] = value_part
+            kv[slot, t * TILE : (t + 1) * TILE, :TILE] = key_part
+            kv[slot, t * TILE : (t + 1) * TILE, TILE:] = value_part
+
+    @pl.when(pair == 0)
+    def _():
+        all_blocks(False)
+        for load in loads:
+            load.wait()
+
+    @pl.when((pair > 0) & (pair < PAIRS))
+    def _():
+        all_blocks(True)
+
+    @pl.when(pair == PAIRS)
+    def _():
+        out_weights()
+        query_weights()
+        for i in range(3):
+            pair_weights(i)
+        for i in range(3):
+            at = slice(i * 256, (i + 1) * 256)
+            qg_out[:, at] = nt(dq_s[...], wq[at, :]).astype(BF16)
+
+
+def attention(lists, counts, order, kw, vw, q, dp, dpt, awt, qft, do, wq):
     blocks = (PAIRS, 16, TILE, TILE)
-    by_pair = pl.BlockSpec((1, 16, TILE, TILE), lambda h, *_: (h, 0, 0, 0))
-    tall = pl.BlockSpec((Q_DEV, TILE), lambda h, *_: (0, h))
-    wide = pl.BlockSpec((TILE, Q_DEV), lambda h, *_: (h, 0))
+    here = lambda p: jnp.minimum(p, PAIRS - 1)
+    past = lambda p: jnp.maximum(p - 1, 0)
+    by_pair = pl.BlockSpec((1, 16, TILE, TILE), lambda p, *_: (here(p), 0, 0, 0))
+    tall = pl.BlockSpec((Q_DEV, TILE), lambda p, *_: (0, here(p)))
+    wide = pl.BlockSpec((TILE, Q_DEV), lambda p, *_: (here(p), 0))
+    any_spec = pl.BlockSpec(memory_space=pl.ANY)
+    vmem = pltpu.VMEM
     return pl.pallas_call(
         attention_kernel,
         name="attention",
         out_shape=[
             jax.ShapeDtypeStruct(blocks, BF16),
             jax.ShapeDtypeStruct(blocks, BF16),
-            jax.ShapeDtypeStruct((D, Q_DEV), BF16),
+            jax.ShapeDtypeStruct((2, 3, D, HALF), BF16),
+            jax.ShapeDtypeStruct((D, D), BF16),
             jax.ShapeDtypeStruct((Q_DEV, D), BF16),
         ],
         grid_spec=pltpu.PrefetchScalarGridSpec(
             num_scalar_prefetch=3,
-            grid=(PAIRS,),
-            in_specs=[by_pair, by_pair, tall, tall, wide],
-            out_specs=[by_pair, by_pair, wide, tall],
-            scratch_shapes=[pltpu.VMEM((16, TILE, TILE), F32), pltpu.VMEM((16, TILE, TILE), F32)],
+            grid=(PAIRS + 1,),
+            in_specs=[by_pair, by_pair, tall, tall, wide] + [any_spec] * 4,
+            out_specs=[
+                by_pair,
+                by_pair,
+                pl.BlockSpec((1, 3, D, TILE), lambda p, *_: (past(p) // 3, 0, 0, past(p) % 3)),
+                pl.BlockSpec((TILE, D), lambda p, *_: (past(p), 0)),
+                pl.BlockSpec((Q_DEV, D), lambda p, *_: (0, 0)),
+            ],
+            scratch_shapes=[
+                vmem((16, TILE, TILE), F32), vmem((16, TILE, TILE), F32),
+                vmem((2, 16 * TILE, 2 * TILE), BF16), vmem((2, TILE, Q_DEV), BF16),
+                vmem((Q_DEV, D), BF16), vmem((D, 16 * TILE), BF16), vmem((D, Q_DEV), BF16),
+                vmem((Q_DEV, D), BF16), vmem((D, D), BF16), pltpu.SemaphoreType.DMA((4,)),
+            ],
         ),
         compiler_params=pltpu.CompilerParams(vmem_limit_bytes=VMEM_BYTES),
-    )(lists, counts, order, kw, vw, q, dp, dpt)
+    )(lists, counts, order, kw, vw, q, dp, dpt, awt, qft, do, wq)
 
 
 def grads_kernel(
     extents,
-    pk_in, pv_in, awt_in, qft_in, att_in, dq_in, do_in, wq_in, wk_in, wv_in,
-    ag_out, qg_out, wg_out,
-    pk, pv, awt, qft, att, dq, do, wq, wk, wv,
-    corner, passed, ends, end_s, end_r, side_s, side_r, corner_r, acc, qg_s, ag_s, wg_s,
-    mine, core_s, core_r, term, yf, yrl, ysum, xf, xrl, xsum,
-    ta, tb, xa_r, yb_r, zs, zr, fs, fr,
+    pk_in, pv_in, w_in, wo_in, wk_in, wv_in,
+    ag_out, wg_out,
+    pk, pv, wk, wv,
+    corner, passed, ends, end_s, end_r, side_s, side_r, corner_r, acc, ag_s, wg_s,
+    mine, core_r, term, yf, yrl, ysum, xf, xrl, xsum,
+    ta, tb, xa_r, yb_r, zs, zr,
     load_sem, store_sem, pass_send, pass_recv, end_send, end_recv, side_send, side_recv,
     cs_sem, cr_sem, ys_sem, yr_sem, xs_sem, xr_sem, xas_sem, xar_sem, ybs_sem, ybr_sem,
-    zs_sem, zr_sem, f_sem,
+    zs_sem, zr_sem,
 ):
     gx, gy = lax.axis_index("gx"), lax.axis_index("gy")
     core = lax.rem(gy, 2)
@@ -373,15 +479,20 @@
     pairs = [(wk_in, wk), (wv_in, wv)]
     for at in groups:
         pairs += [(pk_in.at[:, at], pk.at[:, at]), (pv_in.at[:, at], pv.at[:, at])]
-    pairs += [(qft_in, qft), (dq_in, dq), (att_in, att), (do_in, do), (awt_in, awt), (wq_in, wq)]
+    def terms_in(m, half):
+        if m < 3:
+            return w_in.at[half, m]
+        return wo_in.at[:, pl.ds(pl.multiple_of(half * HALF, 128), HALF)]
+
+    pairs += [(terms_in(m, core), mine.at[m]) for m in range(4)]
     loads = [pltpu.make_async_copy(s, d, load_sem.at[i]) for i, (s, d) in enumerate(pairs)]
-    for load in loads:
+    for load in loads[0:4] + loads[10:14] + loads[4:10]:
         load.start()
     sibling = device(y, x, z, 1 - core)
     fixed = [sibling]
     fixed += [device(lax.rem(y + k, 4), x, z, core) for k in (1, 2, 3)]
     fixed += [device(y, lax.rem(x + k, 4), z, core) for k in (1, 2, 3)]
-    fixed += [device(y, x, lax.rem(z + k, 8), core) for k in range(1, 8)]
+    fixed += [device(y, x, lax.rem(z + k, 8), c) for k in range(1, 8) for c in (0, 1)]
     greet([((gx + dx, gy + dy), exists(dx, dy)) for dx, dy in DIRS]
           + [(where, gx >= 0) for where in fixed])
 
@@ -413,7 +524,7 @@
     def from_corner(rx, ry, direct):
         n, p = int(rx == 1), int(ry == 1)
         dst = corner_r.at[n] if direct else passed.at[n, 1 - p]
-        return remote(corner.at[2 * n + p], dst, pass_send.at[n, p], pass_recv.at[n, 1 - p],
+        return remote(corner.at[2 * p + n], dst, pass_send.at[n, p], pass_recv.at[n, 1 - p],
                       (gx + (rx if direct else 0), gy + ry))
 
     def from_end(rx, c):
@@ -426,73 +537,59 @@
         return remote(side_s.at[2 * p : 2 * p + 2], side_r.at[p], side_send.at[p],
                       side_recv.at[p], (gx, gy + ry))
 
-    for load in loads[0:4]:
-        load.wait()
-    terms_of(3, corner)
-    for rx, ry in ((-1, 1), (1, -1), (-1, -1), (1, 1)):
-        direct = straight(-rx, -ry, gy + ry)
-
-        @pl.when(exists(rx, ry) & direct)
-        def _(rx=rx, ry=ry):
-            from_corner(rx, ry, True).start()
-
-        @pl.when(exists(rx, ry) & jnp.logical_not(direct))
-        def _(rx=rx, ry=ry):
-            from_corner(rx, ry, False).start()
-    for load in loads[4:6]:
-        load.wait()
-    terms_of(2, ends)
-    for load in loads[6:8]:
-        load.wait()
-    terms_of(1, side_s)
-    first = jnp.where(gy < 2, 0, 1)
-    for turn in range(2):
-        c = first if turn == 0 else 1 - first
-        for rx in (-1, 1):
-            n = int(rx == 1)
-            waits = jnp.where(
-                c == 0,
-                exists(rx, -1) & jnp.logical_not(straight(-rx, -1, gy)),
-                exists(rx, 1) & jnp.logical_not(straight(-rx, 1, gy)),
-            )
-
-            @pl.when(exists(rx, 0) & waits)
-            def _(rx=rx, n=n, c=c):
-                remote(corner.at[0], passed.at[n, c], pass_send.at[0, 0], pass_recv.at[n, c],
-                       sibling).wait_recv()
-                end_s[2 * n + c] = (ends[2 * n + c] + passed[n, c].astype(F32)).astype(BF16)
-
-            @pl.when(exists(rx, 0) & jnp.logical_not(waits))
-            def _(n=n, c=c):
-                end_s[2 * n + c] = ends[2 * n + c].astype(BF16)
-
-            @pl.when(exists(rx, 0))
-            def _(rx=rx, c=c):
-                from_end(rx, c).start()
-    for ry in (-1, 1):
-        @pl.when(exists(0, ry))
-        def _(ry=ry):
-            from_side(ry).start()
+    need = {
+        "C": (0, 1, 2, 3), "E": (0, 1, 4, 5), "S": (0, 1, 6, 7), "K": (0, 1, 8, 9),
+        "A0": (10,), "A1": (11,), "A2": (12,), "A3": (13,),
+    }
+
+    def corner_terms():
+        terms_of(3, corner)
+        for rx, ry in ((-1, 1), (1, -1), (-1, -1), (1, 1)):
+            direct = straight(-rx, -ry, gy + ry)
+
+            @pl.when(exists(rx, ry) & direct)
+            def _(rx=rx, ry=ry):
+                from_corner(rx, ry, True).start()
+
+            @pl.when(exists(rx, ry) & jnp.logical_not(direct))
+            def _(rx=rx, ry=ry):
+                from_corner(rx, ry, False).start()
+
+    def send_ends():
+        first = jnp.where(gy < 2, 0, 1)
+        for turn in range(2):
+            c = first if turn == 0 else 1 - first
+            for rx in (-1, 1):
+                n = int(rx == 1)
+                waits = jnp.where(
+                    c == 0,
+                    exists(rx, -1) & jnp.logical_not(straight(-rx, -1, gy)),
+                    exists(rx, 1) & jnp.logical_not(straight(-rx, 1, gy)),
+                )
+
+                @pl.when(exists(rx, 0) & waits)
+                def _(rx=rx, n=n, c=c):
+                    remote(corner.at[0], passed.at[n, c], pass_send.at[0, 0],
+                           pass_recv.at[n, c], sibling).wait_recv()
+                    end_s[2 * n + c] = (ends[2 * n + c] + passed[n, c].astype(F32)).astype(BF16)
+
+                @pl.when(exists(rx, 0) & jnp.logical_not(waits))
+                def _(n=n, c=c):
+                    end_s[2 * n + c] = ends[2 * n + c].astype(BF16)
+
+                @pl.when(exists(rx, 0))
+                def _(rx=rx, c=c):
+                    from_end(rx, c).start()
+
+    def side_terms():
+        terms_of(1, side_s)
+        for ry in (-1, 1):
+            @pl.when(exists(0, ry))
+            def _(ry=ry):
+                from_side(ry).start()
 
     def crossing(m):
-        return remote(core_s.at[m], core_r.at[m], cs_sem.at[m], cr_sem.at[m], sibling)
-
-    def weight_halves(m, rows_of, columns_of):
-        def step(n, _):
-            half = jnp.where(n == 0, 1 - core, core)
-            part = nn(rows_of(), columns_of(half))
-
-            @pl.when(n == 0)
-            def _():
-                core_s[m] = part.astype(BF16)
-                crossing(m).start()
-
-            @pl.when(n == 1)
-            def _():
-                mine[m] = part
-            return 0
-
-        lax.fori_loop(0, 2, step, 0)
+        return remote(terms_in(m, 1 - core), core_r.at[m], cs_sem.at[m], cr_sem.at[m], sibling)
 
     y_up, y_down = device(lax.rem(y + 1, 4), x, z, core), device(lax.rem(y + 3, 4), x, z, core)
     x_next, x_over, x_last = lax.rem(x + 1, 4), lax.rem(x + 2, 4), lax.rem(x + 3, 4)
@@ -530,7 +627,9 @@
         for goal in range(4):
             for part in range(2):
                 at = slice(goal * 192 + part * 96, goal * 192 + part * 96 + 96)
-                term[m, goal, part] = (mine[m, at] + core_r[m, at].astype(F32)).astype(BF16)
+                term[m, goal, part] = (
+                    mine[m, at].astype(F32) + core_r[m, at].astype(F32)
+                ).astype(BF16)
 
         @pl.when(y_place(m) == 2)
         def _():
@@ -540,6 +639,7 @@
         for i in (2, 3):
             x_copy(m, i).start()
 
+    def send_next(m):
         @pl.when(y_place(m) == 1)
         def _():
             y_copy(m, 0).start()
@@ -578,45 +678,26 @@
             ).astype(BF16)
             x_copy(m, 4 + n).start()
 
-    def lanes(ref, half):
-        return ref[:, pl.ds(pl.multiple_of(half * HALF, 128), HALF)]
-
-    def stacked(ref, half):
-        return jnp.concatenate(
-            [ref[half * 3 + i].reshape(16 * TILE, TILE) for i in range(3)], axis=1
-        )
-
-    def anchor_rows():
-        return jnp.concatenate([awt[t] for t in range(16)], axis=1)
-
-    for load in loads[10:14]:
-        load.wait()
-    weight_halves(0, lambda: qft[...], lambda half: lanes(dq, half))
-    weight_halves(3, lambda: att[...], lambda half: lanes(do, half))
-    add_cores(0)
-    for load in loads[8:10] + loads[14:15]:
-        load.wait()
-    weight_halves(1, anchor_rows, lambda half: stacked(pk, half))
-    add_cores(3)
-    hand_on(0)
-    weight_halves(2, anchor_rows, lambda half: stacked(pv, half))
-    add_cores(1)
-    hand_on(3)
-    add_cores(2)
-
-    terms_of(0, acc)
-    hand_on(1)
-    loads[15].wait()
-
-    def query_grad(j, _):
-        at = pl.ds(pl.multiple_of(j * 256, 256), 256)
-        qg_s[:, at] = nt(dq[...], wq[at, :]).astype(BF16)
-        return 0
-
-    lax.fori_loop(0, 3, query_grad, 0)
-    qg_copy = pltpu.make_async_copy(qg_s, qg_out, store_sem.at[0])
-    qg_copy.start()
-    hand_on(2)
+    steps = {
+        "C": corner_terms, "E": lambda: terms_of(2, ends), "G": send_ends, "S": side_terms,
+        "K": lambda: terms_of(0, acc),
+    }
+    for m in range(4):
+        steps["A%d" % m] = partial(add_cores, m)
+        steps["B%d" % m] = partial(send_next, m)
+        steps["H%d" % m] = partial(hand_on, m)
+    def cross():
+        for m in range(4):
+            crossing(m).start()
+
+    steps["X"] = cross
+    loaded = set()
+    for step in ORDER:
+        for i in need.get(step, ()):
+            if i not in loaded:
+                loaded.add(i)
+                loads[i].wait()
+        steps[step]()
 
     for i in (0, 1, 4, 5):
         y_copy(0, i).wait_recv()
@@ -645,29 +726,40 @@
     for k in (2, 1, 3):
         to_row_second(k).start()
 
-    zs[:, 16:32] = jnp.zeros((8, 16, HALF), BF16)
+    zs[...] = jnp.zeros((8, 2, 16, HALF), BF16)
+
+    def cut(total, base):
+        for i in range(4):
+            for c in range(2):
+                row = i * 24 + c * 12
+                zs[base + i, c, 0:12] = total[row : row + 12].astype(BF16)
+
     for k in (1, 2, 3):
         to_column_second(k).wait_recv()
     total = ta[x].astype(F32)
     for slot in range(3):
         total = total + xa_r[slot].astype(F32)
-    for i in range(4):
-        zs[i, 0:24] = total[i * 24 : (i + 1) * 24].astype(BF16)
+    cut(total, 0)
     for k in (1, 2, 3):
         to_row_second(k).wait_recv()
     total = tb[y].astype(F32)
     for slot in range(3):
         total = total + yb_r[slot].astype(F32)
-    for i in range(4):
-        zs[4 + i, 0:24] = total[i * 24 : (i + 1) * 24].astype(BF16)
-
-    def along(k):
+    cut(total, 4)
+
+    def along(k, c):
         goal = lax.rem(z + k, 8)
-        return remote(zs.at[goal], zr.at[7 - k], zs_sem.at[k - 1], zr_sem.at[7 - k],
-                      device(y, x, goal, core))
+        return remote(zs.at[goal, c], zr.at[core, 7 - k], zs_sem.at[k, c], zr_sem.at[core, 7 - k],
+                      device(y, x, goal, c))
+
+    def across():
+        return remote(zs.at[z, 1 - core], zr.at[core, 7], zs_sem.at[0, 0], zr_sem.at[core, 7],
+                      sibling)
 
     for k in (4, 3, 5, 2, 6, 1, 7):
-        along(k).start()
+        for c in (0, 1):
+            along(k, c).start()
+    across().start()
 
     for ry in (-1, 1):
         @pl.when(exists(0, -ry))
@@ -695,26 +787,26 @@
             acc[2 * r + c] += corner_r[n].astype(F32)
 
     ag_s[...] = acc[...].astype(BF16)
-    ag_copy = pltpu.make_async_copy(ag_s, ag_out, store_sem.at[1])
+    ag_copy = pltpu.make_async_copy(ag_s, ag_out, store_sem.at[0])
     ag_copy.start()
 
-    for k in range(1, 8):
-        along(k).wait_recv()
-    total = zs[z].astype(F32)
+    def arrived(c, slot):
+        remote(zs.at[0, 0], zr.at[c, slot], zs_sem.at[0, 0], zr_sem.at[c, slot],
+               sibling).wait_recv()
+        return zr[c, slot].astype(F32)
+
+    held = zs[z, core].astype(F32)
     for slot in range(7):
-        total = total + zr[slot].astype(F32)
-    fs[...] = total[0:24]
-    last = remote(fs, fr, f_sem.at[0], f_sem.at[1], sibling)
-    last.start()
-    last.wait()
+        held = held + arrived(core, slot)
+    other = arrived(1 - core, 7)
+    for slot in range(7):
+        other = other + arrived(1 - core, slot)
     low = core == 0
-    held, other = fs[...], fr[...]
-    held = jnp.where(low, held[0:12], held[12:24])
-    other = jnp.where(low, other[0:12], other[12:24])
+    held, other = held[0:12], other[0:12]
     norm = (extents[0] * extents[1] * Q_DEV) ** (-0.5)
     wg_s[:, 0:HALF] = jnp.where(low, held, other) * norm
     wg_s[:, HALF:D] = jnp.where(low, other, held) * norm
-    wg_copy = pltpu.make_async_copy(wg_s, wg_out, store_sem.at[2])
+    wg_copy = pltpu.make_async_copy(wg_s, wg_out, store_sem.at[1])
     wg_copy.start()
 
     for rx in (-1, 1):
@@ -739,50 +831,79 @@
         to_column_second(k).wait_send()
         to_row_second(k).wait_send()
     for k in range(1, 8):
-        along(k).wait_send()
-    qg_copy.wait()
+        for c in (0, 1):
+            along(k, c).wait_send()
+    across().wait_send()
     ag_copy.wait()
     wg_copy.wait()
 
 
-def grads(extents, pk, pv, awt, qft, att, dq, do, wq, wk, wv):
+def grads(extents, pk, pv, w, wo, wk, wv):
     any_spec = pl.BlockSpec(memory_space=pl.ANY)
     blocks = (PAIRS, 16, TILE, TILE)
-    tall, wide, square = (Q_DEV, D), (D, Q_DEV), (D, D)
+    square = (D, D)
     four, two = (4, TILE, D), (2, 2, TILE, D)
     dma = pltpu.SemaphoreType.DMA
     held = [
-        (blocks, BF16), (blocks, BF16), ((16, D, TILE), BF16), (wide, BF16), (wide, BF16),
-        (tall, BF16), (tall, BF16), (square, BF16), (square, BF16), (square, BF16),
+        (blocks, BF16), (blocks, BF16), (square, BF16), (square, BF16),
         (four, BF16), (two, BF16), (four, F32), (four, BF16), (two, BF16), (four, BF16),
-        (two, BF16), ((2, TILE, D), BF16), (four, F32), (tall, BF16), (four, BF16),
+        (two, BF16), ((2, TILE, D), BF16), (four, F32), (four, BF16),
         ((12, D), F32),
-        ((4, D, HALF), F32), ((4, D, HALF), BF16), ((4, D, HALF), BF16),
+        ((4, D, HALF), BF16), ((4, D, HALF), BF16),
         ((4, 4, 2, 96, HALF), BF16),
         ((2, 4, 96, HALF), BF16), ((2, 2, 96, HALF), BF16), ((2, 2, 96, HALF), BF16),
         ((4, 2, 96, HALF), BF16), ((4, 2, 48, HALF), BF16), ((4, 2, 48, HALF), BF16),
         ((4, 96, HALF), BF16), ((4, 96, HALF), BF16), ((3, 96, HALF), BF16),
-        ((3, 96, HALF), BF16), ((8, 32, HALF), BF16), ((7, 32, HALF), BF16),
-        ((24, HALF), F32), ((24, HALF), F32),
+        ((3, 96, HALF), BF16), ((8, 2, 16, HALF), BF16), ((2, 8, 16, HALF), BF16),
     ]
-    sems = [(16,), (3,), (2, 2), (2, 2), (2, 2), (2, 2), (2,), (2,), (4,), (4,), (6,), (6,),
-            (4, 6), (4, 6), (3,), (3,), (3,), (3,), (7,), (7,), (2,)]
-    anchor_grad, query_grad, weight_grads = pl.pallas_call(
+    sems = [(14,), (2,), (2, 2), (2, 2), (2, 2), (2, 2), (2,), (2,), (4,), (4,), (6,), (6,),
+            (4, 6), (4, 6), (3,), (3,), (3,), (3,), (8, 2), (2, 8)]
+    anchor_grad, weight_grads = pl.pallas_call(
         partial(grads_kernel, extents),
         name="grads",
         out_shape=[
             jax.ShapeDtypeStruct(four, BF16),
-            jax.ShapeDtypeStruct(tall, BF16),
             jax.ShapeDtypeStruct((12, D), F32),
         ],
-        in_specs=[any_spec] * 10,
-        out_specs=[any_spec] * 3,
+        in_specs=[any_spec] * 6,
+        out_specs=[any_spec] * 2,
         scratch_shapes=[pltpu.VMEM(s, t) for s, t in held] + [dma(s) for s in sems],
         compiler_params=pltpu.CompilerParams(
             collective_id=1, has_side_effects=True, vmem_limit_bytes=VMEM_BYTES
         ),
-    )(pk, pv, awt, qft, att, dq, do, wq, wk, wv)
-    return anchor_grad.reshape(2, 2, TILE, D), query_grad, weight_grads
+    )(pk, pv, w, wo, wk, wv)
+    return anchor_grad, weight_grads
+
+
+def settle_kernel(ag_in, wg_in, ag_out, wg_out, ag, wg, sem):
+    loads = [
+        pltpu.make_async_copy(ag_in.at[n], ag.at[n], sem.at[0, n]) for n in range(4)
+    ] + [pltpu.make_async_copy(wg_in, wg, sem.at[0, 4])]
+    stores = [
+        pltpu.make_async_copy(ag.at[n], ag_out.at[n], sem.at[1, n]) for n in range(4)
+    ] + [pltpu.make_async_copy(wg, wg_out, sem.at[1, 4])]
+    for load in loads:
+        load.start()
+    for load, store in zip(loads, stores):
+        load.wait()
+        store.start()
+    for store in stores:
+        store.wait()
+
+
+def settle(anchor_grad, weight_grads):
+    any_spec = pl.BlockSpec(memory_space=pl.ANY)
+    held = (anchor_grad, weight_grads)
+    return pl.pallas_call(
+        settle_kernel,
+        name="settle",
+        out_shape=[jax.ShapeDtypeStruct(h.shape, h.dtype) for h in held],
+        in_specs=[any_spec] * 2,
+        out_specs=[any_spec] * 2,
+        scratch_shapes=[pltpu.VMEM(h.shape, h.dtype) for h in held]
+        + [pltpu.SemaphoreType.DMA((2, 5))],
+        compiler_params=pltpu.CompilerParams(vmem_limit_bytes=VMEM_BYTES),
+    )(*held)
 
 
 def on_device(
@@ -793,11 +914,11 @@
     do = out_grad.reshape(Q_DEV, D)
     order = jnp.array([HELD.index((w // 4, w % 4)) for w in range(16)], jnp.int32)
     kw, vw, awt, q, dp, dpt, qft = halo(extents, anchors, qf, do, w_query, w_key, w_value, w_out)
-    pk, pv, att, dq = attention(tile_lists, tile_counts, order, kw, vw, q, dp, dpt)
-    anchor_grad, query_grad, weight_grads = grads(
-        extents, pk, pv, awt, qft, att, dq, do, w_query, w_key, w_value
+    pk, pv, w, wo, query_grad = attention(
+        tile_lists, tile_counts, order, kw, vw, q, dp, dpt, awt, qft, do, w_query
     )
-    return query_grad.reshape(query_feats.shape), anchor_grad, weight_grads
+    anchor_grad, weight_grads = settle(*grads(extents, pk, pv, w, wo, w_key, w_value))
+    return query_grad.reshape(query_feats.shape), anchor_grad.reshape(anchors.shape), weight_grads
 
 
 def solution(mesh):

time: 128 us -> 110 us (0.86)
  Pallas kernels: 122 us -> 108 us
  local copies, waits for them, and re-layouts: 4.76 us -> 0 us
    pallas_call x1, Pallas kernels: 56.8 us -> 43.4 us  [grads(): pl.pallas_call(partial(grads_kernel, extents), name='grads', out_shape=[j...]
    unnamed x5 -> x0, local copies, waits for them, and re-layouts: 4.76 us -> none
    pallas_call x0 -> x1, Pallas kernels: none -> 1.99 us  [settle(): pl.pallas_call(settle_kernel, name='settle', out_shape=[jax.ShapeDtypeStr...]
    pallas_call x1, Pallas kernels: 27 us -> 25.4 us  [attention(): pl.pallas_call(attention_kernel, name='attention', out_shape=[jax.ShapeDt...]
where the time goes in v3:
time: 110 us; the launch traced here: 109 us
  Pallas kernels  108 us (98%)
    pallas_call x1, Pallas kernels, grads(): pl.pallas_call(partial(grads_kernel, extents), name='grads', out_shape=[j...  43.4 us
    pallas_call x1, Pallas kernels, halo(): pl.pallas_call(partial(halo_kernel, extents), name='halo', out_shape=[jax...  37.5 us
    pallas_call x1, Pallas kernels, attention(): pl.pallas_call(attention_kernel, name='attention', out_shape=[jax.ShapeDt...  25.4 us

profile of v3, /device:TPU:1, one launch (start us, length us, event | category | flops | bytes accessed | tf_op | source)
XLA Modules:
  0.0 109.1 jit_solution(17508679948291589005)
XLA Ops:
  0.6 37.5 %halo.1 = (bf16[6,16,128,128]{3,2,1,0:T(8,128)(2,1)}, bf16[6,16,128,128]{3,2,1,0:T(8,128)(2,1)}, bf16[768,2048]{1,0:T(8,128)(2,1)}, bf16[512,768]{1,0:T(8,128)(2...) custom-call(bf16[2,2,128,768]{3,2,1,0:T(8,128)(2,1)} %anchors.1, ...), custom_call_target="tpu_custom_call" | custom-call | tf_op jit(solution)/shard_map/halo/pallas_call | solution.py:253
  38.2 25.4 %attention.1 = (bf16[6,16,128,128]{3,2,1,0:T(8,128)(2,1)}, bf16[6,16,128,128]{3,2,1,0:T(8,128)(2,1)}, bf16[2,3,768,384]{3,2,1,0:T(8,128)(2,1)}, bf16[768,768]{1,0:T(8,128)(2,1)}, bf16[512,768]{1,0:T(8,128)(2,1)}) custom-call(s32[1,1,4,4]{3,2,1,0:T(4,128)} %lists.1, s32[1,1,4]{2,1,0:T(1,128)} %counts.1, s32[16]{0:T(128)} %constant.2.clone.order, ...), custom_call_target="tpu_custom_call" | custom-call | tf_op jit(solution)/shard_map/attention/pallas_call | solution.py:422
  63.6 43.4 %grads.1 = (bf16[4,128,768]{2,1,0:T(8,128)(2,1)}, f32[12,768]{1,0:T(8,128)}) custom-call(bf16[6,16,128,128]{3,2,1,0:T(8,128)(2,1)} %get-tuple-element.27.pk_in, bf16[6,16,128,128]{3,2,1,0:T(8,128)(2,1)} %get-tuple-element.28.pv_in, bf16[2,3,768,384]{3,2,1,0:T(8,128)(2,1)} %get-tuple-element.29.w_in, bf16[768,768]{1,0:T(8,128)(2,1)} %get-tuple-element.30.wo_in, ...), custom_call_target="tpu_custom_call" | custom-call | tf_op jit(solution)/shard_map/grads/pallas_call | solution.py:861
  107.0 2.0 %settle.1 = (bf16[4,128,768]{2,1,0:T(8,128)(2,1)}, f32[12,768]{1,0:T(8,128)}) custom-call(bf16[4,128,768]{2,1,0:T(8,128)(2,1)} %get-tuple-element.31.ag_in, f32[12,768]{1,0:T(8,128)} %get-tuple-element.32.wg_in), custom_call_target="tpu_custom_call" | custom-call | tf_op jit(solution)/shard_map/settle/pallas_call | solution.py:897

commit v4 on v3

--- a/solution.py
+++ b/solution.py
@@ -19,8 +19,8 @@
 LOG2E = 1.4426950408889634
 DEAD = 1e30
 ORDER = (
-    "X", "C", "A0", "B0", "A1", "B1", "E", "A2", "B2", "A3", "B3", "G", "H0", "H1", "S", "H2", "H3",
-    "K",
+    "X", "C", "A0", "B0", "A1", "B1", "S", "A2", "B2", "A3", "B3", "E", "G", "H0", "H1", "H2", "H3",
+    "Y", "L0", "L1", "L2", "L3", "K", "Z",
 )
 MESH = pl.DeviceIdType.MESH
 F32 = jnp.float32
@@ -188,7 +188,7 @@
                         ]
             return 0
 
-        lax.fori_loop(0, 3, step, 0)
+        lax.fori_loop(0, 3, step, 0, unroll=True)
         for n, (r, c) in enumerate(places):
             awt[:, pl.ds(pl.multiple_of((base + n) * TILE, TILE), TILE)] = win[r, c].T
         at = pl.ds(base, count)
@@ -486,7 +486,7 @@
 
     pairs += [(terms_in(m, core), mine.at[m]) for m in range(4)]
     loads = [pltpu.make_async_copy(s, d, load_sem.at[i]) for i, (s, d) in enumerate(pairs)]
-    for load in loads[0:4] + loads[10:14] + loads[4:10]:
+    for load in loads[0:4] + loads[6:8] + loads[10:14] + loads[4:6] + loads[8:10]:
         load.start()
     sibling = device(y, x, z, 1 - core)
     fixed = [sibling]
@@ -691,6 +691,73 @@
             crossing(m).start()
 
     steps["X"] = cross
+    def to_column_second(k):
+        goal = lax.rem(x + k, 4)
+        return remote(ta.at[goal], xa_r.at[3 - k], xas_sem.at[k - 1], xar_sem.at[3 - k],
+                      device(y, goal, z, core))
+
+    def to_row_second(m):
+        slot = lax.rem(7 - y_place(m), 4)
+        return remote(tb.at[m], yb_r.at[slot], ybs_sem.at[m], ybr_sem.at[slot],
+                      device(m, x, z, core))
+
+    def second_of_rows():
+        for i in (0, 1, 4, 5):
+            y_copy(0, i).wait_recv()
+        for goal in range(4):
+            total = term[y, goal, 0].astype(F32)
+            ta[goal] = (total + yf[0, goal].astype(F32) + yf[1, goal].astype(F32)).astype(BF16)
+        for k in (2, 1, 3):
+            to_column_second(k).start()
+
+    def second_of_columns(m):
+        for i in (0, 1, 4, 5):
+            x_copy(m, i).wait_recv()
+        total = term[m, x, 1].astype(F32)
+        tb[m] = (total + xf[m, 0].astype(F32) + xf[m, 1].astype(F32)).astype(BF16)
+
+        @pl.when(y != m)
+        def _():
+            to_row_second(m).start()
+
+    def cut(total, base):
+        for i in range(4):
+            for c in range(2):
+                row = i * 24 + c * 12
+                block = jnp.concatenate([total[row : row + 12], jnp.zeros((4, HALF), F32)], axis=0)
+                zs[base + i, c] = block.astype(BF16)
+
+    def along(k, c):
+        goal = lax.rem(z + k, 8)
+        return remote(zs.at[goal, c], zr.at[core, 7 - k], zs_sem.at[k, c], zr_sem.at[core, 7 - k],
+                      device(y, x, goal, c))
+
+    def across():
+        return remote(zs.at[z, 1 - core], zr.at[core, 7], zs_sem.at[0, 0], zr_sem.at[core, 7],
+                      sibling)
+
+    def third():
+        for k in (1, 2, 3):
+            to_column_second(k).wait_recv()
+        total = ta[x].astype(F32)
+        for slot in range(3):
+            total = total + xa_r[slot].astype(F32)
+        cut(total, 0)
+        for slot in range(3):
+            remote(tb.at[0], yb_r.at[slot], ybs_sem.at[0], ybr_sem.at[slot], sibling).wait_recv()
+        total = tb[y].astype(F32)
+        for slot in range(3):
+            total = total + yb_r[slot].astype(F32)
+        cut(total, 4)
+        for k in (4, 3, 5, 2, 6, 1, 7):
+            for c in (0, 1):
+                along(k, c).start()
+        across().start()
+
+    steps["Y"], steps["Z"] = second_of_rows, third
+    for m in range(4):
+        steps["L%d" % m] = partial(second_of_columns, m)
+
     loaded = set()
     for step in ORDER:
         for i in need.get(step, ()):
@@ -698,68 +765,6 @@
                 loaded.add(i)
                 loads[i].wait()
         steps[step]()
-
-    for i in (0, 1, 4, 5):
-        y_copy(0, i).wait_recv()
-    for goal in range(4):
-        total = term[y, goal, 0].astype(F32)
-        ta[goal] = (total + yf[0, goal].astype(F32) + yf[1, goal].astype(F32)).astype(BF16)
-
-    def to_column_second(k):
-        goal = lax.rem(x + k, 4)
-        return remote(ta.at[goal], xa_r.at[3 - k], xas_sem.at[k - 1], xar_sem.at[3 - k],
-                      device(y, goal, z, core))
-
-    for k in (2, 1, 3):
-        to_column_second(k).start()
-    for m in range(4):
-        for i in (0, 1, 4, 5):
-            x_copy(m, i).wait_recv()
-        total = term[m, x, 1].astype(F32)
-        tb[m] = (total + xf[m, 0].astype(F32) + xf[m, 1].astype(F32)).astype(BF16)
-
-    def to_row_second(k):
-        goal = lax.rem(y + k, 4)
-        return remote(tb.at[goal], yb_r.at[3 - k], ybs_sem.at[k - 1], ybr_sem.at[3 - k],
-                      device(goal, x, z, core))
-
-    for k in (2, 1, 3):
-        to_row_second(k).start()
-
-    zs[...] = jnp.zeros((8, 2, 16, HALF), BF16)
-
-    def cut(total, base):
-        for i in range(4):
-            for c in range(2):
-                row = i * 24 + c * 12
-                zs[base + i, c, 0:12] = total[row : row + 12].astype(BF16)
-
-    for k in (1, 2, 3):
-        to_column_second(k).wait_recv()
-    total = ta[x].astype(F32)
-    for slot in range(3):
-        total = total + xa_r[slot].astype(F32)
-    cut(total, 0)
-    for k in (1, 2, 3):
-        to_row_second(k).wait_recv()
-    total = tb[y].astype(F32)
-    for slot in range(3):
-        total = total + yb_r[slot].astype(F32)
-    cut(total, 4)
-
-    def along(k, c):
-        goal = lax.rem(z + k, 8)
-        return remote(zs.at[goal, c], zr.at[core, 7 - k], zs_sem.at[k, c], zr_sem.at[core, 7 - k],
-                      device(y, x, goal, c))
-
-    def across():
-        return remote(zs.at[z, 1 - core], zr.at[core, 7], zs_sem.at[0, 0], zr_sem.at[core, 7],
-                      sibling)
-
-    for k in (4, 3, 5, 2, 6, 1, 7):
-        for c in (0, 1):
-            along(k, c).start()
-    across().start()
 
     for ry in (-1, 1):
         @pl.when(exists(0, -ry))
@@ -829,7 +834,10 @@
             x_copy(m, i).wait_send()
     for k in (1, 2, 3):
         to_column_second(k).wait_send()
-        to_row_second(k).wait_send()
+    for m in range(4):
+        @pl.when(y != m)
+        def _(m=m):
+            to_row_second(m).wait_send()
     for k in range(1, 8):
         for c in (0, 1):
             along(k, c).wait_send()
@@ -857,7 +865,7 @@
         ((3, 96, HALF), BF16), ((8, 2, 16, HALF), BF16), ((2, 8, 16, HALF), BF16),
     ]
     sems = [(14,), (2,), (2, 2), (2, 2), (2, 2), (2, 2), (2,), (2,), (4,), (4,), (6,), (6,),
-            (4, 6), (4, 6), (3,), (3,), (3,), (3,), (8, 2), (2, 8)]
+            (4, 6), (4, 6), (3,), (3,), (4,), (3,), (8, 2), (2, 8)]
     anchor_grad, weight_grads = pl.pallas_call(
         partial(grads_kernel, extents),
         name="grads",

time: 110 us -> 109 us (level)
  no operation moved by 1% of the time
where the time goes in v4:
time: 109 us; the launch traced here: 108 us
  Pallas kernels  108 us (99%)
    pallas_call x1, Pallas kernels, grads(): pl.pallas_call(partial(grads_kernel, extents), name='grads', out_shape=[j...  43.4 us
    pallas_call x1, Pallas kernels, halo(): pl.pallas_call(partial(halo_kernel, extents), name='halo', out_shape=[jax...  36.6 us
    pallas_call x1, Pallas kernels, attention(): pl.pallas_call(attention_kernel, name='attention', out_shape=[jax.ShapeDt...  25.6 us

profile of v4, /device:TPU:1, one launch (start us, length us, event | category | flops | bytes accessed | tf_op | source)
XLA Modules:
  0.0 108.4 jit_solution(3038947727837810396)
XLA Ops:
  0.6 36.6 %halo.1 = (bf16[6,16,128,128]{3,2,1,0:T(8,128)(2,1)}, bf16[6,16,128,128]{3,2,1,0:T(8,128)(2,1)}, bf16[768,2048]{1,0:T(8,128)(2,1)}, bf16[512,768]{1,0:T(8,128)(2...) custom-call(bf16[2,2,128,768]{3,2,1,0:T(8,128)(2,1)} %anchors.1, ...), custom_call_target="tpu_custom_call" | custom-call | tf_op jit(solution)/shard_map/halo/pallas_call | solution.py:253
  37.2 25.6 %attention.1 = (bf16[6,16,128,128]{3,2,1,0:T(8,128)(2,1)}, bf16[6,16,128,128]{3,2,1,0:T(8,128)(2,1)}, bf16[2,3,768,384]{3,2,1,0:T(8,128)(2,1)}, bf16[768,768]{1,0:T(8,128)(2,1)}, bf16[512,768]{1,0:T(8,128)(2,1)}) custom-call(s32[1,1,4,4]{3,2,1,0:T(4,128)} %lists.1, s32[1,1,4]{2,1,0:T(1,128)} %counts.1, s32[16]{0:T(128)} %constant.2.clone.order, ...), custom_call_target="tpu_custom_call" | custom-call | tf_op jit(solution)/shard_map/attention/pallas_call | solution.py:422
  62.8 43.4 %grads.1 = (bf16[4,128,768]{2,1,0:T(8,128)(2,1)}, f32[12,768]{1,0:T(8,128)}) custom-call(bf16[6,16,128,128]{3,2,1,0:T(8,128)(2,1)} %get-tuple-element.27.pk_in, bf16[6,16,128,128]{3,2,1,0:T(8,128)(2,1)} %get-tuple-element.28.pv_in, bf16[2,3,768,384]{3,2,1,0:T(8,128)(2,1)} %get-tuple-element.29.w_in, bf16[768,768]{1,0:T(8,128)(2,1)} %get-tuple-element.30.wo_in, ...), custom_call_target="tpu_custom_call" | custom-call | tf_op jit(solution)/shard_map/grads/pallas_call | solution.py:869
  106.2 2.0 %settle.1 = (bf16[4,128,768]{2,1,0:T(8,128)(2,1)}, f32[12,768]{1,0:T(8,128)}) custom-call(bf16[4,128,768]{2,1,0:T(8,128)(2,1)} %get-tuple-element.31.ag_in, f32[12,768]{1,0:T(8,128)} %get-tuple-element.32.wg_in), custom_call_target="tpu_custom_call" | custom-call | tf_op jit(solution)/shard_map/settle/pallas_call | solution.py:905

commit v5 on v4

--- a/solution.py
+++ b/solution.py
@@ -53,14 +53,21 @@
     return (px >= 0) & (px < nx) & (py >= 0) & (py < ny)
 
 
-def greet(partners):
+def greet(partners, meanwhile):
     barrier = pltpu.get_barrier_semaphore()
     total = jnp.int32(0)
     for where, present in partners:
+        if present is True:
+            pl.semaphore_signal(barrier, inc=1, device_id=where, device_id_type=MESH)
+            total = total + 1
+            continue
+
         @pl.when(present)
-        def _():
+        def _(where=where):
             pl.semaphore_signal(barrier, inc=1, device_id=where, device_id_type=MESH)
         total = total + jnp.where(present, 1, 0).astype(jnp.int32)
+    for copy in meanwhile:
+        copy.start()
     pl.semaphore_wait(barrier, total)
 
 
@@ -83,10 +90,10 @@
         )
     ]
     own = pltpu.make_async_copy(anchors, win.at[1:3, 1:3], load_sem.at[6])
-    for load in loads:
-        load.start()
-    own.start()
-    greet([((gx + dx, gy + dy), inside((gx + dx, gy + dy), extents)) for dx, dy in DIRS])
+    greet(
+        [((gx + dx, gy + dy), inside((gx + dx, gy + dy), extents)) for dx, dy in DIRS],
+        loads + [own],
+    )
 
     def exists(dx, dy):
         return inside((gx + dx, gy + dy), extents)
@@ -486,15 +493,14 @@
 
     pairs += [(terms_in(m, core), mine.at[m]) for m in range(4)]
     loads = [pltpu.make_async_copy(s, d, load_sem.at[i]) for i, (s, d) in enumerate(pairs)]
-    for load in loads[0:4] + loads[6:8] + loads[10:14] + loads[4:6] + loads[8:10]:
-        load.start()
     sibling = device(y, x, z, 1 - core)
     fixed = [sibling]
     fixed += [device(lax.rem(y + k, 4), x, z, core) for k in (1, 2, 3)]
     fixed += [device(y, lax.rem(x + k, 4), z, core) for k in (1, 2, 3)]
     fixed += [device(y, x, lax.rem(z + k, 8), c) for k in range(1, 8) for c in (0, 1)]
     greet([((gx + dx, gy + dy), exists(dx, dy)) for dx, dy in DIRS]
-          + [(where, gx >= 0) for where in fixed])
+          + [(where, True) for where in fixed],
+          loads[0:4] + loads[6:8] + loads[10:14] + loads[4:6] + loads[8:10])
 
     def remote(src, dst, send, recv, where):
         return pltpu.make_async_remote_copy(

time: 109 us -> 109 us (level)
  no operation moved by 1% of the time
where the time goes in v5:
time: 109 us; the launch traced here: 108 us
  Pallas kernels  108 us (99%)
    pallas_call x1, Pallas kernels, grads(): pl.pallas_call(partial(grads_kernel, extents), name='grads', out_shape=[j...  43.3 us
    pallas_call x1, Pallas kernels, halo(): pl.pallas_call(partial(halo_kernel, extents), name='halo', out_shape=[jax...  36.6 us
    pallas_call x1, Pallas kernels, attention(): pl.pallas_call(attention_kernel, name='attention', out_shape=[jax.ShapeDt...  25.6 us

profile of v5, /device:TPU:1, one launch (start us, length us, event | category | flops | bytes accessed | tf_op | source)
XLA Modules:
  0.0 108.3 jit_solution(9016452445150225540)
XLA Ops:
  0.6 36.6 %halo.1 = (bf16[6,16,128,128]{3,2,1,0:T(8,128)(2,1)}, bf16[6,16,128,128]{3,2,1,0:T(8,128)(2,1)}, bf16[768,2048]{1,0:T(8,128)(2,1)}, bf16[512,768]{1,0:T(8,128)(2...) custom-call(bf16[2,2,128,768]{3,2,1,0:T(8,128)(2,1)} %anchors.1, ...), custom_call_target="tpu_custom_call" | custom-call | tf_op jit(solution)/shard_map/halo/pallas_call | solution.py:260
  37.2 25.6 %attention.1 = (bf16[6,16,128,128]{3,2,1,0:T(8,128)(2,1)}, bf16[6,16,128,128]{3,2,1,0:T(8,128)(2,1)}, bf16[2,3,768,384]{3,2,1,0:T(8,128)(2,1)}, bf16[768,768]{1,0:T(8,128)(2,1)}, bf16[512,768]{1,0:T(8,128)(2,1)}) custom-call(s32[1,1,4,4]{3,2,1,0:T(4,128)} %lists.1, s32[1,1,4]{2,1,0:T(1,128)} %counts.1, s32[16]{0:T(128)} %constant.2.clone.order, ...), custom_call_target="tpu_custom_call" | custom-call | tf_op jit(solution)/shard_map/attention/pallas_call | solution.py:429
  62.9 43.3 %grads.1 = (bf16[4,128,768]{2,1,0:T(8,128)(2,1)}, f32[12,768]{1,0:T(8,128)}) custom-call(bf16[6,16,128,128]{3,2,1,0:T(8,128)(2,1)} %get-tuple-element.27.pk_in, bf16[6,16,128,128]{3,2,1,0:T(8,128)(2,1)} %get-tuple-element.28.pv_in, bf16[2,3,768,384]{3,2,1,0:T(8,128)(2,1)} %get-tuple-element.29.w_in, bf16[768,768]{1,0:T(8,128)(2,1)} %get-tuple-element.30.wo_in, ...), custom_call_target="tpu_custom_call" | custom-call | tf_op jit(solution)/shard_map/grads/pallas_call | solution.py:875
  106.2 2.0 %settle.1 = (bf16[4,128,768]{2,1,0:T(8,128)(2,1)}, f32[12,768]{1,0:T(8,128)}) custom-call(bf16[4,128,768]{2,1,0:T(8,128)(2,1)} %get-tuple-element.31.ag_in, f32[12,768]{1,0:T(8,128)} %get-tuple-element.32.wg_in), custom_call_target="tpu_custom_call" | custom-call | tf_op jit(solution)/shard_map/settle/pallas_call | solution.py:911
